TPU v7x, 32 devices: a whole 2x2x4 slice. The times are simulated.
32 devices in a mesh: seq: 16 (over z, y, core), chan: 2 (over x).
Axes of the slice: x: 2, y: 2, z: 4, core: 2. Of those that a mesh axis runs over, the one named last changes fastest.
Arguments:
- tokens: bfloat16 [2, 4096, 1536], P(None, 'seq'), may hold values from -6 to 6
- gain_mix: float32 [1536], replicated, may hold values from 0.25 to 1.75
- w_in: bfloat16 [3, 1536, 1536], P(None, None, 'chan'), may hold values from -0.15625 to 0.15625
- kernel: float32 [3, 1536], P(None, 'chan'), may hold values from -3 to 3
- w_out: bfloat16 [1536, 1536], P('chan'), may hold values from -0.15625 to 0.15625
- gain_ffn: float32 [1536], replicated, may hold values from 0.25 to 1.75
- w_gate: bfloat16 [1536, 6912], P(None, 'chan'), may hold values from -0.15625 to 0.15625
- w_up: bfloat16 [1536, 6912], P(None, 'chan'), may hold values from -0.15625 to 0.15625
- w_down: bfloat16 [6912, 1536], P('chan'), may hold values from -0.078125 to 0.078125
- cotangent: bfloat16 [2, 4096, 1536], P(None, 'seq'), may hold values from -6 to 6
Outputs:
- block_out: bfloat16 [2, 4096, 1536], P(None, 'seq')
- d_tokens: bfloat16 [2, 4096, 1536], P(None, 'seq')
- g_gain_mix: float32 [1536], P('seq')
- g_w_in: float32 [3, 1536, 1536], P(None, 'seq', 'chan')
- g_kernel: float32 [3, 2, 768], P(None, 'chan', 'seq')
- g_w_out: float32 [1536, 1536], P('chan', 'seq')
- g_gain_ffn: float32 [1536], P('seq')
- g_w_gate: float32 [1536, 6912], P('seq', 'chan')
- g_w_up: float32 [1536, 6912], P('seq', 'chan')
- g_w_down: float32 [6912, 1536], P('chan', 'seq')
All inputs are finite; a program needn't handle non-finite values.
Results may differ from a plain program's by a relative error of at most 0.017.
Values may be sent and summed in bfloat16 or wider, within the bound.
A program may use at most 320 MiB of HBM per device.

v0:
```python
import jax
import jax.numpy as jnp
from jax import lax
from jax.sharding import PartitionSpec as P

epsilon = 1e-05


def from_behind(value, axis, by):
    count = lax.axis_size(axis)
    pairs = [(i, i + by) for i in range(count) if 0 <= i + by < count]
    return lax.ppermute(value, axis, pairs)


def rms_scale(vector):
    return lax.rsqrt(jnp.mean(vector * vector, axis=-1, keepdims=True) + epsilon)


def norm_back(d_normout, normed, inv_scale, gain_vec):
    d_normed = d_normout * gain_vec
    return inv_scale * (d_normed - normed * jnp.mean(d_normed * normed, axis=-1, keepdims=True))


def matmul(lhs_mat, rhs_mat):
    return jnp.dot(lhs_mat, rhs_mat, preferred_element_type=jnp.float32)


def left_trans(lhs_mat, rhs_mat):
    return lax.dot_general(
        lhs_mat, rhs_mat, (((0,), (0,)), ((), ())), preferred_element_type=jnp.float32
    )


def right_trans(lhs_mat, rhs_mat):
    return lax.dot_general(
        lhs_mat, rhs_mat, (((1,), (1,)), ((), ())), preferred_element_type=jnp.float32
    )


def body(tokens, gain_mix, w_in, kernel, w_out, gain_ffn, w_gate, w_up, w_down, cotangent):
    seq_count, tok_rows, model_width = tokens.shape
    row_count = seq_count * tok_rows
    tokens_f = tokens.astype(jnp.float32).reshape(row_count, model_width)
    scale_mix = rms_scale(tokens_f)
    normed_mix = tokens_f * scale_mix
    h_mix = (normed_mix * gain_mix).astype(jnp.bfloat16)
    proj_b = matmul(h_mix, w_in[0])
    proj_c = matmul(h_mix, w_in[1])
    proj_x = matmul(h_mix, w_in[2])
    conv_in = (proj_b * proj_x).astype(jnp.bfloat16).reshape(seq_count, tok_rows, -1)
    before = from_behind(conv_in[:, tok_rows - 2 :, :], "seq", 1)
    extended = jnp.concatenate([before, conv_in], axis=1).astype(jnp.float32)
    conv_out = (
        kernel[0] * extended[:, :-2] + kernel[1] * extended[:, 1:-1] + kernel[2] * extended[:, 2:]
    )
    conv_flat = conv_out.reshape(row_count, -1)
    gated = (proj_c * conv_flat).astype(jnp.bfloat16)
    mixed_sum = lax.psum(matmul(gated, w_out).astype(jnp.bfloat16), "chan").astype(jnp.float32)
    residual = tokens_f + mixed_sum
    scale_ffn = rms_scale(residual)
    normed_ffn = residual * scale_ffn
    h_ffn = (normed_ffn * gain_ffn).astype(jnp.bfloat16)
    gate_pre = matmul(h_ffn, w_gate)
    up_value = matmul(h_ffn, w_up)
    sigmoid_gate = jax.nn.sigmoid(gate_pre)
    silu_gate = gate_pre * sigmoid_gate
    hidden = (silu_gate * up_value).astype(jnp.bfloat16)
    ffn_total = lax.psum(matmul(hidden, w_down).astype(jnp.bfloat16), "chan").astype(jnp.float32)
    block_out = (
        (residual + ffn_total).astype(jnp.bfloat16).reshape(seq_count, tok_rows, model_width)
    )
    grad_out = cotangent.reshape(row_count, model_width)
    g_w_down = left_trans(hidden, grad_out)
    d_hidden = right_trans(grad_out, w_down)
    d_gate = (d_hidden * up_value * sigmoid_gate * (1.0 + gate_pre * (1.0 - sigmoid_gate))).astype(
        jnp.bfloat16
    )
    d_up = (d_hidden * silu_gate).astype(jnp.bfloat16)
    g_w_gate = left_trans(h_ffn, d_gate)
    g_w_up = left_trans(h_ffn, d_up)
    d_h_ffn = lax.psum(
        (right_trans(d_gate, w_gate) + right_trans(d_up, w_up)).astype(jnp.bfloat16), "chan"
    ).astype(jnp.float32)
    g_gain_ffn = jnp.sum(d_h_ffn * normed_ffn, axis=0)
    d_resid = grad_out.astype(jnp.float32) + norm_back(d_h_ffn, normed_ffn, scale_ffn, gain_ffn)
    d_mixed = d_resid.astype(jnp.bfloat16)
    g_w_out = left_trans(gated, d_mixed)
    d_gated = right_trans(d_mixed, w_out)
    d_proj_c = (d_gated * conv_flat).astype(jnp.bfloat16)
    d_conv = (d_gated * proj_c).reshape(seq_count, tok_rows, -1)
    after_rows = from_behind(d_conv[:, :2, :], "seq", -1)
    ext_back = jnp.concatenate([d_conv, after_rows], axis=1)
    d_conv_in = (
        kernel[2] * ext_back[:, :-2] + kernel[1] * ext_back[:, 1:-1] + kernel[0] * ext_back[:, 2:]
    )
    g_kernel = jnp.stack(
        [
            jnp.sum(d_conv * extended[:, :-2], axis=(0, 1)),
            jnp.sum(d_conv * extended[:, 1:-1], axis=(0, 1)),
            jnp.sum(d_conv * extended[:, 2:], axis=(0, 1)),
        ]
    ).reshape(3, 1, -1)
    d_conv_low = d_conv_in.reshape(row_count, -1).astype(jnp.bfloat16)
    d_proj_b = (d_conv_low * proj_x).astype(jnp.bfloat16)
    d_proj_x = (d_conv_low * proj_b).astype(jnp.bfloat16)
    g_w_in = jnp.stack(
        [left_trans(h_mix, d_proj_b), left_trans(h_mix, d_proj_c), left_trans(h_mix, d_proj_x)]
    )
    d_h_mix = lax.psum(
        (
            right_trans(d_proj_b, w_in[0])
            + right_trans(d_proj_c, w_in[1])
            + right_trans(d_proj_x, w_in[2])
        ).astype(jnp.bfloat16),
        "chan",
    ).astype(jnp.float32)
    g_gain_mix = jnp.sum(d_h_mix * normed_mix, axis=0)
    d_tokens = (
        (d_resid + norm_back(d_h_mix, normed_mix, scale_mix, gain_mix))
        .astype(jnp.bfloat16)
        .reshape(seq_count, tok_rows, model_width)
    )
    summed = (
        lax.psum_scatter(g_w_in, "seq", scatter_dimension=1, tiled=True),
        lax.psum_scatter(g_w_out, "seq", scatter_dimension=1, tiled=True),
        lax.psum_scatter(g_kernel, "seq", scatter_dimension=2, tiled=True),
        lax.psum_scatter(g_gain_mix, "seq", scatter_dimension=0, tiled=True),
        lax.psum_scatter(g_w_gate, "seq", scatter_dimension=0, tiled=True),
        lax.psum_scatter(g_w_up, "seq", scatter_dimension=0, tiled=True),
        lax.psum_scatter(g_w_down, "seq", scatter_dimension=1, tiled=True),
        lax.psum_scatter(g_gain_ffn, "seq", scatter_dimension=0, tiled=True),
    )
    sum_in, sum_out, sum_kernel, sum_gain_mix, sum_gate, sum_up, sum_down, sum_gain_ffn = summed
    return (
        block_out,
        d_tokens,
        sum_gain_mix,
        sum_in,
        sum_kernel,
        sum_out,
        sum_gain_ffn,
        sum_gate,
        sum_up,
        sum_down,
    )


def solution(mesh):
    placed = (
        P(None, "seq", None),
        P(),
        P(None, None, "chan"),
        P(None, "chan"),
        P("chan", None),
        P(),
        P(None, "chan"),
        P(None, "chan"),
        P("chan", None),
        P(None, "seq", None),
    )
    return jax.shard_map(
        body,
        mesh=mesh,
        in_specs=placed,
        out_specs=(
            P(None, "seq", None),
            P(None, "seq", None),
            P("seq"),
            P(None, "seq", "chan"),
            P(None, "chan", "seq"),
            P("chan", "seq"),
            P("seq"),
            P("seq", "chan"),
            P("seq", "chan"),
            P("chan", "seq"),
        ),
        check_vma=False,
    )
```

profile of v0, /device:TPU:0, one launch (start us, length us, event | category | flops | bytes accessed | tf_op | source)
XLA Modules:
  0.0 1248.0 jit_solution(7793167548650534202)
XLA Ops:
  11.4 3.2 fusion.24
  14.7 2.5 multiply_convert_fusion.4
  21.7 2.5 fusion.47
  24.3 2.6 convolution_convert_fusion.1
  27.1 55.9 %all-reduce.8.cloned.1.call-done = bf16[512,1536]{1,0:T(8,128)(2,1)} async-done(((bf16[512,1536]{1,0:T(8,128)(2,1)}), bf16[512,1536]{1,0:T(8,128)(2,1)}) %all-reduce.8.cloned.1.call-update) | async-done | bytes 1572880 | tf_op jit(solution)/shard_map/psum | solution.py:58
  83.0 2.6 multiply_reduce_fusion
  86.4 12.9 %fusion.55 = f32[512,3456]{1,0:T(8,128)} fusion(bf16[512,1536]{1,0:T(8,128)(2,1)S(1)} %multiply_convert_fusion.3, bf16[1536,3456]{1,0:T(8,128)(2,1)} %param.17), kind=kOutput, calls=%fused_computation.102 | convolution fusion | flops 5435817984 | bytes 19267584 | tf_op jit(solution)/shard_map/dot_general | solution.py:25
  99.4 7.8 fusion.54
  107.3 17.5 %multiply_convert_fusion = (bf16[512,3456]{1,0:T(8,128)(2,1)}, bf16[512,3456]{1,0:T(8,128)(2,1)}, bf16[512,3456]{1,0:T(8,128)(2,1)}) fusion(f32[512,3456]{1,0:T(8,128)} %fusion.54, f32[512,3456]{1,0:T(8,128)} %fusion.55, bf16[512,1536]{1,0:T(8,128)(2,1)} %bitcast.119, bf16[3456,1536]{1,0:T(8,128)(2,1)} %param.18), kind=kOutput, calls=%fused_computation.1 | convolution fusion | flops 5462360064 | bytes 36962304 | tf_op jit(solution)/shard_map/dot_general | solution.py:35
  124.7 9.8 fusion.56
  134.6 9.5 fusion.20
  144.4 10.5 convolution_convert_fusion
  154.9 40.9 %all-reduce.10.cloned.1.call-done = bf16[512,1536]{1,0:T(8,128)(2,1)} async-done(((bf16[512,1536]{1,0:T(8,128)(2,1)}), bf16[512,1536]{1,0:T(8,128)(2,1)}) %all-reduce.10.cloned.1.call-update) | async-done | bytes 1572880 | tf_op jit(solution)/shard_map/psum | solution.py:81
  195.8 3.8 fusion.12
  199.6 2.8 fusion.11
  211.3 2.6 fusion.21
  216.9 5.7 fusion.49
  222.7 78.7 %all-reduce.12.cloned.1.call-done = (bf16[512,1536]{1,0:T(8,128)(2,1)}, bf16[512,1536]{1,0:T(8,128)(2,1)}) async-done(((bf16[512,1536]{1,0:T(8,128)(2,1)}, bf16[512,1536]{1,0:T(8,128)(2,1)}), (bf16[512,1536]{1,0:T(8,128)(2,1)}, bf16[512,1536]{1,0:T(8,128)(2,1)})) %all-reduce.12.cloned.1.call-update) | async-done | bytes 3145744 | tf_op jit(solution)/shard_map/psum | solution.py:68
  301.5 2.6 fusion.13
  304.1 5.0 fusion.16
  309.1 3.6 convolution_bitcast_fusion
  312.6 3.6 convolution_bitcast_fusion.1
  316.2 3.7 convolution_bitcast_fusion.2
  319.9 11.1 pad_maximum_fusion
  332.5 12.2 fusion.58
  344.9 12.2 fusion.57
  358.5 12.4 fusion.59
  374.4 62.4 %all-reduce.2 = (f32[1536]{0:T(1024)S(1)}, f32[1536]{0:T(1024)S(1)}) all-reduce(f32[1536]{0:T(1024)S(1)} %get-tuple-element.15, f32[1536]{0:T(1024)S(1)} %get-tuple-element.10), channel_id=2, replica_groups=mesh['seq'=16,'chan'=2] {'seq'}, use_global_device_ids=true, to_apply=%region_9.0.clone | all-reduce | flops 3072 | bytes 24576
  440.2 149.8 %reduce-scatter.9.cloned.1.call-done = f32[3,96,768]{2,1,0:T(8,128)} async-done(((f32[3,1536,768]{2,1,0:T(8,128)}), f32[3,96,768]{2,1,0:T(8,128)}) %reduce-scatter.9.cloned.1.call-update) | async-done | bytes 884752 | tf_op jit(solution)/shard_map/reduce_scatter | solution.py:124
  590.0 217.2 %reduce-scatter.15.cloned.1.call-done = f32[96,3456]{1,0:T(8,128)} async-done(((f32[1536,3456]{1,0:T(8,128)}), f32[96,3456]{1,0:T(8,128)}) %reduce-scatter.15.cloned.1.call-update) | async-done | bytes 1327120 | tf_op jit(solution)/shard_map/reduce_scatter | solution.py:129
  807.2 216.7 %reduce-scatter.13.cloned.1.call-done = f32[96,3456]{1,0:T(8,128)} async-done(((f32[1536,3456]{1,0:T(8,128)}), f32[96,3456]{1,0:T(8,128)}) %reduce-scatter.13.cloned.1.call-update) | async-done | bytes 1327120 | tf_op jit(solution)/shard_map/reduce_scatter | solution.py:128
  1023.9 217.3 %reduce-scatter.17.cloned.1.call-done = f32[3456,96]{0,1:T(8,128)} async-done(((f32[3456,1536]{0,1:T(8,128)}), f32[3456,96]{0,1:T(8,128)}) %reduce-scatter.17.cloned.1.call-update) | async-done | bytes 1327120 | tf_op jit(solution)/shard_map/reduce_scatter | solution.py:130
  (132 shorter events, 31.0 us)
Async XLA Ops:
  7.2 17.1 %copy-start = (bf16[768,1536]{1,0:T(8,128)(2,1)S(1)}, bf16[768,1536]{1,0:T(8,128)(2,1)}, u32[]{:S(2)}) copy-start(bf16[768,1536]{1,0:T(8,128)(2,1)} %param.14) | copy-start | bytes 7077892
  7.2 75.8 %all-reduce.8.cloned.1.call-start = ((), (), s32[]{:S(2)}) async-start(), calls=%async_computation.6 | async-start | bytes 3145728 | tf_op jit(solution)/shard_map/psum | solution.py:58
  7.2 7.4 slice-start
  11.4 3.2 slice-start.1
  14.7 4.9 copy-start.27
  17.2 3.2 collective-permute-start
  26.8 58.8 %copy-start.26 = (f32[1536]{0:T(1024)S(1)}, f32[1536]{0:T(1024)}, u32[]{:S(2)}) copy-start(f32[1536]{0:T(1024)} %param.15) | copy-start | bytes 18436
  26.9 168.9 %all-reduce.10.cloned.1.call-start = ((), (), s32[]{:S(2)}) async-start(), calls=%async_computation.7 | async-start | bytes 3145728 | tf_op jit(solution)/shard_map/psum | solution.py:81
  85.8 13.6 %slice-start.4 = ((s8[10616832]{0:T(1024)(128)(4,1)}), s8[4194304]{0:T(1024)(128)(4,1)S(1)}, s32[]{:S(2)}) async-start(s8[10616832]{0:T(1024)(128)(4,1)} %bitcast.134), calls=%async_computation.19 | async-start | bytes 8388608
  86.4 13.0 %copy-start.16 = (bf16[512,1536]{1,0:T(8,128)(2,1)}, bf16[512,1536]{1,0:T(8,128)(2,1)S(1)}, u32[]{:S(2)}) copy-start(bf16[512,1536]{1,0:T(8,128)(2,1)S(1)} %multiply_convert_fusion.3) | copy-start | bytes 4718596
  86.4 13.0 %slice-start.5 = ((s8[10616832]{0:T(1024)(128)(4,1)}), s8[4194304]{0:T(1024)(128)(4,1)S(1)}, s32[]{:S(2)}) async-start(s8[10616832]{0:T(1024)(128)(4,1)} %bitcast.134), calls=%async_computation.20 | async-start | bytes 8388608
  86.4 13.0 %slice-start.6 = ((s8[10616832]{0:T(1024)(128)(4,1)}), s8[2228224]{0:T(1024)(128)(4,1)S(1)}, s32[]{:S(2)}) async-start(s8[10616832]{0:T(1024)(128)(4,1)} %bitcast.134), calls=%async_computation.21 | async-start | bytes 4456448
  124.7 9.8 copy-start.29
  144.1 157.3 %all-reduce.12.cloned.1.call-start = ((), (), s32[]{:S(2)}) async-start(), calls=%async_computation.14 | async-start | bytes 6291456 | tf_op jit(solution)/shard_map/psum | solution.py:68
  195.8 3.8 copy-start.3
  195.8 3.8 copy-start.8
  195.8 3.8 copy-start.11
  199.6 8.8 slice-start.2
  202.5 3.2 copy-start.13
  202.5 6.0 slice-start.3
  204.2 3.2 collective-permute-start.1
  214.0 158.9 %reduce-scatter.19.cloned.1.call-start = ((), (), s32[]{:S(2)}) async-start(), calls=%async_computation.13 | async-start | bytes 417792
  216.5 223.7 %reduce-scatter.11.cloned.1.call-start = ((), (), s32[]{:S(2)}) async-start(), calls=%async_computation.9 | async-start | bytes 5013504 | tf_op jit(solution)/shard_map/reduce_scatter | solution.py:125
  222.7 78.8 %copy-start.4 = (bf16[2,256,1536]{2,1,0:T(8,128)(2,1)S(1)}, bf16[2,256,1536]{2,1,0:T(8,128)(2,1)}, u32[]{:S(2)}) copy-start(bf16[2,256,1536]{2,1,0:T(8,128)(2,1)} %param.10) | copy-start | bytes 4718596
  222.7 78.8 %copy-start.25 = (f32[1536]{0:T(1024)S(1)}, f32[1536]{0:T(1024)}, u32[]{:S(2)}) copy-start(f32[1536]{0:T(1024)} %param.11) | copy-start | bytes 18436
  222.7 367.3 %reduce-scatter.9.cloned.1.call-start = ((), (), s32[]{:S(2)}) async-start(), calls=%async_computation.8 | async-start | bytes 15040512 | tf_op jit(solution)/shard_map/reduce_scatter | solution.py:124
  304.1 5.0 copy-start.24
  312.6 3.6 copy-start.22
  331.1 476.2 %reduce-scatter.15.cloned.1.call-start = ((), (), s32[]{:S(2)}) async-start(), calls=%async_computation.11 | async-start | bytes 22560768 | tf_op jit(solution)/shard_map/reduce_scatter | solution.py:129
  344.7 679.3 %reduce-scatter.13.cloned.1.call-start = ((), (), s32[]{:S(2)}) async-start(), calls=%async_computation.10 | async-start | bytes 22560768 | tf_op jit(solution)/shard_map/reduce_scatter | solution.py:128
  357.1 884.1 %reduce-scatter.17.cloned.1.call-start = ((), (), s32[]{:S(2)}) async-start(), calls=%async_computation.12 | async-start | bytes 22560768 | tf_op jit(solution)/shard_map/reduce_scatter | solution.py:130
  371.0 870.3 %copy-start.1 = (bf16[768,1536]{1,0:T(8,128)(2,1)S(1)}, bf16[768,1536]{1,0:T(8,128)(2,1)}, u32[]{:S(2)}) copy-start(bf16[768,1536]{1,0:T(8,128)(2,1)} %param.14) | copy-start | bytes 7077892
  (16 other events, 34.4 us)
Sparse Core Ops, SparseCore 0:
  27.0 55.9 all-reduce.7
  144.2 51.4 all-reduce.9
  214.1 87.3 all-reduce.11
  305.2 55.5 reduce-scatter.18
  365.1 75.0 reduce-scatter.10
  445.4 144.6 reduce-scatter.8
  595.3 211.8 reduce-scatter.14
  811.9 211.9 reduce-scatter.12
  1029.2 211.9 reduce-scatter.16
where the time goes:
time: 1250 us
  waiting for transfers between devices  981 us (78%)
  matrix products  139 us (11%)
  blocking collectives  62.4 us (5%)
  other arithmetic  34.4 us (3%)
  between operations  15.3 us (1%)
    reduce_scatter x1, waiting for transfers between devices, body(): lax.psum_scatter(g_w_down, 'seq', scatter_dimension=1, tiled=True)  217 us
    reduce_scatter x1, waiting for transfers between devices, body(): lax.psum_scatter(g_w_up, 'seq', scatter_dimension=0, tiled=True)  217 us
    reduce_scatter x1, waiting for transfers between devices, body(): lax.psum_scatter(g_w_gate, 'seq', scatter_dimension=0, tiled=True)  217 us
    reduce_scatter x1, waiting for transfers between devices, body(): lax.psum_scatter(g_w_in, 'seq', scatter_dimension=1, tiled=True)  150 us
    psum x1, waiting for transfers between devices, body(): lax.psum(matmul(hidden, w_down).astype(jnp.bfloat16), 'chan')  78.7 us
    unnamed x1, blocking collectives  62.4 us
    psum x1, waiting for transfers between devices, body(): lax.psum(matmul(gated, w_out).astype(jnp.bfloat16), 'chan')  55.9 us
    dot_general x7, matrix products, left_trans(): lax.dot_general(lhs_mat, rhs_mat, (((0,), (0,)), ((), ())), preferred_ele...  53.3 us
  transfers between devices with their start and end apart: 11, of which 10 were waited for; matrix products, arithmetic and copies ran while one was open for 7% of the time, Pallas kernels for 0%

commit v1 on v0

--- a/solution.py
+++ b/solution.py
@@ -1,9 +1,1055 @@
+import functools
+
 import jax
 import jax.numpy as jnp
 from jax import lax
+from jax.experimental import pallas as pl
+from jax.experimental.pallas import tpu as pltpu
 from jax.sharding import PartitionSpec as P
 
 epsilon = 1e-05
+BF = jnp.bfloat16
+F32 = jnp.float32
+MESH = pl.DeviceIdType.MESH
+LANE = 128
+NZ = 4
+ROWS_CHUNK = 128
+ZF_COLS = 1152
+
+
+def nn(a, b):
+    return jnp.dot(a, b, preferred_element_type=F32)
+
+
+def tn(a, b):
+    return lax.dot_general(a, b, (((0,), (0,)), ((), ())), preferred_element_type=F32)
+
+
+def nt(a, b):
+    return lax.dot_general(a, b, (((1,), (1,)), ((), ())), preferred_element_type=F32)
+
+
+def inv_rms(v):
+    return lax.rsqrt(jnp.mean(v * v, axis=-1, keepdims=True) + epsilon)
+
+
+class Take:
+    def __init__(self, limit):
+        self.used, self.limit = 0, limit
+
+    def __call__(self, count=1):
+        base = self.used
+        self.used += count
+        assert self.used <= self.limit
+        return base
+
+
+N_SEND, N_RECV, N_LOCAL = 128, 192, 64
+
+
+def step_kernel(
+    dims,
+    tokens, gain_mix, w_in, taps, w_out, gain_ffn, w_gate, w_up, w_down, cot,
+    block_out, d_tokens, g_ffn, g_conv, small_out,
+    gb0, gb1, gb2, gb3, gb4, yb0, yb1, yb2, yb3, yb4, zb0, zb1, zb2, zb3, zb4,
+    cr_dh, cr_dn, xr_dh, xr_dn, xr_d1,
+    tok_v, wg_v, wu_v, wd_v, dy_v, h2_v, h1_v, hid, dg, du, pb, pc, px, bx, gated, resid, mix_r,
+    ring, rb, ld, outs, halo_s, halo_r, dhalo_s, dhalo_r, tail, pb_tail, px_tail,
+    sm, sm_r, ss, rs, ls,
+):
+    R, T, D, CL, FL, FW = dims
+    S = R // T
+    CH = CL // 2
+    GR = D // NZ
+    SR = GR // 2
+    DR = SR // 2
+    NCH = R // ROWS_CHUNK
+    take_s, take_r, take_l = Take(N_SEND), Take(N_RECV), Take(N_LOCAL)
+
+    s = lax.axis_index("seq")
+    x = lax.axis_index("chan")
+    n_seq = 4 * NZ
+    z, y, c = s // 4, (s // 2) % 2, s % 2
+
+    def did(z_, y_, c_):
+        return ((z_ * 2 + y_) * 2 + c_, x)
+
+    core_dev = did(z, y, 1 - c)
+    y_dev = did(z, 1 - y, c)
+    x_dev = (s, 1 - x)
+    mid = jnp.logical_and(z > 0, z < NZ - 1)
+    end = jnp.logical_not(mid)
+
+    def remote(src, dst, si, ri, dev):
+        return pltpu.make_async_remote_copy(
+            src_ref=src, dst_ref=dst, send_sem=ss.at[si], recv_sem=rs.at[ri],
+            device_id=dev, device_id_type=MESH,
+        )
+
+    def wait_recv(dst, ri):
+        remote(dst, dst, 0, ri, core_dev).wait_recv()
+
+    def wait_send(src, si):
+        remote(src, src, si, 0, core_dev).wait_send()
+
+    def local(src, dst, li):
+        return pltpu.make_async_copy(src, dst, ls.at[li])
+
+    l_tok, l_win, l_wout, l_dy = take_l(), take_l(3), take_l(), take_l()
+    ld_tok = local(tokens, tok_v, l_tok)
+    ld_tok.start()
+    win_views = [wg_v.at[:, pl.ds(0, CL)], wg_v.at[:, pl.ds(CL, CL)], wu_v.at[:, pl.ds(0, CL)]]
+    wout_view = wd_v.at[pl.ds(0, CL), :]
+
+    def load_w_in():
+        return [local(w_in.at[m], win_views[m], l_win + m) for m in range(3)]
+
+    for cp in load_w_in():
+        cp.start()
+    ld_wout = local(w_out, wout_view, l_wout)
+    ld_wout.start()
+    ld_dy = local(cot, dy_v.at[0], l_dy)
+    ld_dy.start()
+
+    bar = pltpu.get_barrier_semaphore()
+
+    def greet(dev):
+        pl.semaphore_signal(bar, inc=1, device_id=dev, device_id_type=MESH)
+
+    greet(core_dev)
+    greet(y_dev)
+    greet(x_dev)
+    for k in range(1, NZ):
+        greet(did((z + k) % NZ, y, c))
+    has_prev = s > 0
+    has_next = s < n_seq - 1
+    prev_dev = ((s + n_seq - 1) % n_seq, x)
+    next_dev = ((s + 1) % n_seq, x)
+    greet(prev_dev)
+    greet(next_dev)
+    pl.semaphore_wait(bar, 4 + NZ)
+
+    s_dy, r_dy = take_s(), take_r()
+    send_dy = remote(cot, dy_v.at[1], s_dy, r_dy, core_dev)
+    send_dy.start()
+
+    sm[...] = jnp.zeros_like(sm)
+    k_taps = [taps[t : t + 1, :] for t in range(3)]
+
+    ld_tok.wait()
+
+    def norm_rows(k, _):
+        rows = pl.ds(pl.multiple_of(k * ROWS_CHUNK, ROWS_CHUNK), ROWS_CHUNK)
+        xv = tok_v[rows, :].astype(F32)
+        h1_v[0, rows, :] = (xv * inv_rms(xv) * gain_mix[...]).astype(BF)
+        return 0
+
+    lax.fori_loop(0, NCH, norm_rows, 0)
+    s_h1, r_h1 = take_s(), take_r()
+    send_h1 = remote(h1_v.at[0], h1_v.at[1], s_h1, r_h1, core_dev)
+    send_h1.start()
+    for cp in load_w_in():
+        cp.wait()
+
+    NC = CL // 256
+
+    def in_proj(j, _):
+        cols = pl.ds(pl.multiple_of(j * 256, 256), 256)
+        cols1 = pl.ds(pl.multiple_of(CL + j * 256, 256), 256)
+        h = h1_v[0]
+        b = nn(h, wg_v[:, cols])
+        pb[:, cols] = b.astype(BF)
+        xx = nn(h, wu_v[:, cols])
+        px[:, cols] = xx.astype(BF)
+        bx[:, cols] = (b * xx).astype(BF)
+        pc[:, cols] = nn(h, wg_v[:, cols1]).astype(BF)
+        return 0
+
+    lax.fori_loop(0, NC, in_proj, 0)
+    l_w = take_l(3)
+    win_start = pl.multiple_of(c * (FL - FW), LANE)
+    ld_wg = local(w_gate.at[:, pl.ds(win_start, FW)], wg_v, l_w)
+    ld_wu = local(w_up.at[:, pl.ds(win_start, FW)], wu_v, l_w + 1)
+    ld_wd = local(w_down.at[pl.ds(win_start, FW), :], wd_v, l_w + 2)
+    ld_wg.start()
+    ld_wu.start()
+
+    s_ha, r_ha = take_s(), take_r()
+    for q in range(S):
+        halo_s[q] = bx[q * T + T - 16 : q * T + T, :]
+    send_halo = remote(halo_s, halo_r, s_ha, r_ha, next_dev)
+
+    @pl.when(has_next)
+    def _():
+        send_halo.start()
+
+    @pl.when(has_prev)
+    def _():
+        wait_recv(halo_r, r_ha)
+
+    @pl.when(jnp.logical_not(has_prev))
+    def _():
+        halo_r[...] = jnp.zeros_like(halo_r)
+
+    row_iota = lax.broadcasted_iota(jnp.int32, (T, 256), 0)
+
+    def conv_terms(q, cols):
+        now = bx[pl.ds(q * T, T), cols].astype(F32)
+        h = halo_r[q, :, cols].astype(F32)
+        h14 = jnp.broadcast_to(h[14:15], now.shape)
+        h15 = jnp.broadcast_to(h[15:16], now.shape)
+        one = jnp.where(row_iota == 0, h15, pltpu.roll(now, 1, 0))
+        two = jnp.where(row_iota == 0, h14, jnp.where(row_iota == 1, h15, pltpu.roll(now, 2, 0)))
+        return now, one, two
+
+    def tap_cols(cols):
+        return [taps[t : t + 1, cols] for t in range(3)]
+
+    ld_wout.wait()
+    s_mx, r_mx = take_s(NCH), take_r(NCH)
+    CPS = T // ROWS_CHUNK
+    for q in range(S):
+
+        def conv_tile(j, _, q=q):
+            cols = pl.ds(pl.multiple_of(j * 256, 256), 256)
+            now, one, two = conv_terms(q, cols)
+            k0, k1, k2 = tap_cols(cols)
+            cv = k0 * two + k1 * one + k2 * now
+            rows = pl.ds(q * T, T)
+            gated[rows, cols] = (pc[rows, cols].astype(F32) * cv).astype(BF)
+            return 0
+
+        lax.fori_loop(0, NC, conv_tile, 0)
+
+        def out_tile(j, _, q=q):
+            cols = pl.ds(pl.multiple_of(j * 512, 512), 512)
+            v = nn(gated[q * T : q * T + T, :], wd_v[0:CL, cols]).astype(BF)
+            ring[q * CPS : q * CPS + CPS, :, cols] = v.reshape(CPS, ROWS_CHUNK, 512)
+            return 0
+
+        lax.fori_loop(0, D // 512, out_tile, 0)
+        for k in range(q * CPS, q * CPS + CPS):
+            remote(ring.at[k], mix_r.at[k], s_mx + k, r_mx + k, x_dev).start()
+    ld_wd.start()
+
+    s_h2, r_h2 = take_s(NCH), take_r(NCH)
+    ld_dy.wait()
+    send_dy.wait()
+    ld_wg.wait()
+    ld_wu.wait()
+    ld_wd.wait()
+    NF = FW // 256
+    overlap = 2 * FW - FL
+    col_iota = lax.broadcasted_iota(jnp.int32, (2 * ROWS_CHUNK, 256), 1)
+
+    def residual_chunk(k):
+        rows = pl.ds(pl.multiple_of(k * ROWS_CHUNK, ROWS_CHUNK), ROWS_CHUNK)
+        wait_recv(mix_r.at[k], r_mx + k)
+        res = tok_v[rows, :].astype(F32) + (ring[k].astype(F32) + mix_r[k].astype(F32))
+        resid[rows, :] = res
+        h2_v[0, rows, :] = (res * inv_rms(res) * gain_ffn[...]).astype(BF)
+        remote(h2_v.at[0, rows], h2_v.at[1, rows], s_h2 + k, r_h2 + k, core_dev).start()
+
+    def ffn_chunk(k):
+        rows = pl.ds(pl.multiple_of(k * ROWS_CHUNK, ROWS_CHUNK), ROWS_CHUNK)
+        wait_recv(h2_v.at[1, rows], r_h2 + k)
+
+        def tile(j, _):
+            cols = pl.ds(pl.multiple_of(j * 256, 256), 256)
+            h = h2_v[:, rows, :].reshape(2 * ROWS_CHUNK, D)
+            e = dy_v[:, rows, :].reshape(2 * ROWS_CHUNK, D)
+            g = nn(h, wg_v[:, cols])
+            u = nn(h, wu_v[:, cols])
+            dh = nt(e, wd_v[cols, :])
+            keep = col_iota + j * 256 >= c * overlap
+            sg = jax.nn.sigmoid(g)
+            si = g * sg
+            dh = jnp.where(keep, dh, 0.0)
+            shape = (2, ROWS_CHUNK, 256)
+            hid[:, rows, cols] = jnp.where(keep, si * u, 0.0).astype(BF).reshape(shape)
+            dg[:, rows, cols] = (dh * u * sg * (1.0 + g * (1.0 - sg))).astype(BF).reshape(shape)
+            du[:, rows, cols] = (dh * si).astype(BF).reshape(shape)
+            return 0
+
+        lax.fori_loop(0, NF, tile, 0)
+
+    residual_chunk(0)
+
+    def chunk_loop(k, _):
+        @pl.when(k + 1 < NCH)
+        def _():
+            residual_chunk(k + 1)
+
+        ffn_chunk(k)
+        return 0
+
+    lax.fori_loop(0, NCH, chunk_loop, 0)
+    for k in range(NCH):
+        wait_send(ring.at[k], s_mx + k)
+        wait_send(h2_v.at[0, pl.ds(k * ROWS_CHUNK, ROWS_CHUNK)], s_h2 + k)
+
+    gbs = [gb0, gb1, gb2, gb3, gb4]
+    ybs = [yb0, yb1, yb2, yb3, yb4]
+    zbs = [zb0, zb1, zb2, zb3, zb4]
+    widths = [ZF_COLS, FW - ZF_COLS, FW, FW, 2 * CL]
+    s_y = [None] + [take_s(NZ) for _ in range(4)]
+    r_y = [None] + [take_r(NZ) for _ in range(4)]
+    s_z = [take_s(2 * NZ)] + [take_s(NZ) for _ in range(4)]
+    r_z = [take_r(4 * NZ)] + [take_r(2 * NZ) for _ in range(4)]
+
+    def order(e):
+        if e == NZ - 1:
+            return z
+        per_z = {0: (3, 2, 1), 1: (3, 0, 2), 2: (0, 3, 1), 3: (0, 1, 2)}
+        v = jnp.int32(per_z[3][e])
+        for zz in range(3):
+            v = jnp.where(z == zz, per_z[zz][e], v)
+        return v
+
+    def order_dyn(u):
+        v = order(NZ - 1)
+        for e in range(NZ - 1):
+            v = jnp.where(u == e, order(e), v)
+        return v
+
+    def z_send(j, src, e, zp, h=None):
+        to_right = zp > z
+        d = jnp.where(to_right, 0, 1)
+        dev = did(jnp.clip(jnp.where(to_right, z + 1, z - 1), 0, NZ - 1), y, c)
+        if h is None:
+            return remote(src, zbs[j].at[d, zp], s_z[j] + e, r_z[j] + d * NZ + zp, dev)
+        return remote(
+            src, zbs[j].at[d, zp, h], s_z[j] + 2 * e + h, r_z[j] + (d * NZ + zp) * 2 + h, dev
+        )
+
+    l_g = take_l(12)
+
+    def g_block(lhs_ref, rhs_ref, zp, pair):
+        lhs = lhs_ref[:, :, pl.ds(pl.multiple_of(zp * GR, GR), GR)].reshape(2 * R, GR)
+        half = FW // 2
+        for n in range(2):
+            v = tn(lhs, rhs_ref[:, :, n * half : (n + 1) * half].reshape(2 * R, half)).astype(BF)
+            outs[2 * pair, :, n * half : (n + 1) * half] = v[:SR]
+            outs[2 * pair + 1, :, n * half : (n + 1) * half] = v[SR:]
+
+    def g_step(u, _):
+        zp = order_dyn(u)
+
+        def down_copies():
+            return [
+                cp
+                for h in range(2)
+                for cp in (
+                    local(outs.at[h, :, pl.ds(0, ZF_COLS)], gb0.at[zp, h], l_g + 2 * h),
+                    local(
+                        outs.at[h, :, pl.ds(ZF_COLS, FW - ZF_COLS)], gb1.at[zp, h], l_g + 2 * h + 1
+                    ),
+                )
+            ]
+
+        def plain_copies(gb, pair, li):
+            return [local(outs.at[2 * pair + h], gb.at[zp, h], li + h) for h in range(2)]
+
+        def y_send(j):
+            remote(gbs[j].at[zp, 1 - y], ybs[j].at[zp], s_y[j] + u, r_y[j] + u, y_dev).start()
+
+        g_block(dy_v, hid, zp, 0)
+        for cp in down_copies():
+            cp.start()
+        g_block(h2_v, dg, zp, 1)
+        for cp in plain_copies(gb2, 1, l_g + 4):
+            cp.start()
+        for cp in down_copies():
+            cp.wait()
+        y_send(1)
+
+        @pl.when(jnp.logical_and(end, u < NZ - 1))
+        def _():
+            for h in range(2):
+                z_send(0, gb0.at[zp, h], u, zp, h).start()
+
+        g_block(h2_v, du, zp, 0)
+        for cp in plain_copies(gb3, 0, l_g + 6):
+            cp.start()
+        for cp in plain_copies(gb2, 1, l_g + 4):
+            cp.wait()
+        y_send(2)
+        for cp in plain_copies(gb3, 0, l_g + 6):
+            cp.wait()
+        y_send(3)
+        return 0
+
+    lax.fori_loop(0, NZ, g_step, 0)
+
+    l_e = take_l(4)
+    slot_last = [None] * outs.shape[0]
+    slot_next = [0]
+
+    def claim_slot():
+        o = slot_next[0]
+        slot_next[0] = (o + 1) % outs.shape[0]
+        if slot_last[o] is not None:
+            slot_last[o]()
+            slot_last[o] = None
+        return o
+
+    ADD_ROWS = 32
+
+    def add_into(dst, srcs):
+        def rows_add(k, _):
+            rows = pl.ds(pl.multiple_of(k * ADD_ROWS, ADD_ROWS), ADD_ROWS)
+            acc = srcs[0][rows, :].astype(F32)
+            for src in srcs[1:]:
+                acc = acc + src[rows, :].astype(F32)
+            dst[rows, :] = acc.astype(BF)
+            return 0
+
+        lax.fori_loop(0, SR // ADD_ROWS, rows_add, 0)
+
+    def add_more(dst, src):
+        def rows_add(k, _):
+            rows = pl.ds(pl.multiple_of(k * ADD_ROWS, ADD_ROWS), ADD_ROWS)
+            dst[rows, :] = (dst[rows, :].astype(F32) + src[rows, :].astype(F32)).astype(BF)
+            return 0
+
+        lax.fori_loop(0, SR // ADD_ROWS, rows_add, 0)
+
+    def line_event(j, e, h=None):
+        zp = order(e)
+        w = widths[j]
+        d = jnp.where(zp > z, 0, 1)
+        la, lb, lc = (ld.at[i, :, pl.ds(0, w)] for i in range(3))
+        if h is None:
+            zsrc, ri = zbs[j].at[d, zp], r_z[j] + d * NZ + zp
+            si = s_z[j] + e
+            o = claim_slot()
+            dst = outs.at[o, :, pl.ds(0, w)]
+            ca = local(gbs[j].at[zp, y], la, l_e)
+            ca.start()
+            wait_recv(ybs[j].at[zp], r_y[j] + e)
+            cb = local(ybs[j].at[zp], lb, l_e + 1)
+            cb.start()
+
+            @pl.when(mid)
+            def _():
+                wait_recv(zsrc, ri)
+                cc = local(zsrc, lc, l_e + 2)
+                cc.start()
+                ca.wait()
+                cb.wait()
+                cc.wait()
+                add_into(dst, [la, lb, lc])
+
+            @pl.when(end)
+            def _():
+                ca.wait()
+                cb.wait()
+                add_into(dst, [la, lb])
+
+            z_send(j, dst, e, zp).start()
+            slot_last[o] = lambda: wait_send(dst, si)
+        else:
+            zsrc, ri = zbs[j].at[d, zp, h], r_z[j] + (d * NZ + zp) * 2 + h
+            si = s_z[j] + 2 * e + h
+            o = claim_slot()
+            dst = outs.at[o, :, pl.ds(0, w)]
+
+            @pl.when(mid)
+            def _():
+                ca = local(gbs[j].at[zp, h], la, l_e)
+                ca.start()
+                wait_recv(zsrc, ri)
+                cc = local(zsrc, lc, l_e + 2)
+                cc.start()
+                ca.wait()
+                cc.wait()
+                add_into(dst, [la, lc])
+                z_send(j, dst, e, zp, h).start()
+
+            def last():
+                @pl.when(mid)
+                def _():
+                    wait_send(dst, si)
+
+            slot_last[o] = last
+
+    def gather_final(j, dst, own, with_y, h=None):
+        w = widths[j]
+        la, lb, lc, ldd = (ld.at[i, :, pl.ds(0, w)] for i in range(4))
+        ca = local(own, la, l_e)
+        ca.start()
+        if with_y:
+            wait_recv(ybs[j].at[z], r_y[j] + NZ - 1)
+            cb = local(ybs[j].at[z], lb, l_e + 1)
+            cb.start()
+
+        def side(d):
+            if h is None:
+                return zbs[j].at[d, z], r_z[j] + d * NZ + z
+            return zbs[j].at[d, z, h], r_z[j] + (d * NZ + z) * 2 + h
+
+        def fetch(d, to, li):
+            src, ri = side(d)
+            wait_recv(src, ri)
+            cp = local(src, to, li)
+            cp.start()
+            return cp
+
+        base = [la, lb] if with_y else [la]
+
+        def finish(cps, srcs):
+            ca.wait()
+            if with_y:
+                cb.wait()
+            for cp in cps:
+                cp.wait()
+            add_into(dst, srcs)
+
+        @pl.when(mid)
+        def _():
+            c0 = fetch(0, lc, l_e + 2)
+            c1 = fetch(1, ldd, l_e + 3)
+            finish([c0, c1], base + [lc, ldd])
+
+        @pl.when(z == 0)
+        def _():
+            c1 = fetch(1, ldd, l_e + 3)
+            finish([c1], base + [ldd])
+
+        @pl.when(z == NZ - 1)
+        def _():
+            c0 = fetch(0, lc, l_e + 2)
+            finish([c0], base + [lc])
+
+    finals = []
+
+    def swap_pieces(j, dst):
+        if j == 4:
+            return [(None, m * CH, CH, g_conv.at[m], c * CH) for m in range(4)]
+        mat = g_ffn.at[{0: 0, 1: 0, 2: 1, 3: 2}[j]]
+        off = ZF_COLS if j == 1 else 0
+        w = widths[j]
+        if j == 1:
+            return [(None, 0, w, mat, c * (FL - FW) + off)]
+        return [(0, 0, w, mat, 0), (1, overlap, w - overlap, mat, FL - FW + overlap)]
+
+    def final_out(j, dst):
+        for cond, c0, w, mat, to in swap_pieces(j, dst):
+            si, ri, li = take_s(), take_r(), take_l()
+            to = pl.multiple_of(to, LANE) if not isinstance(to, int) else to
+            keep = local(
+                dst.at[pl.ds(pl.multiple_of(c * DR, DR), DR), pl.ds(c0, w)],
+                mat.at[:, pl.ds(to, w)], li,
+            )
+            give = remote(
+                dst.at[pl.ds(pl.multiple_of((1 - c) * DR, DR), DR), pl.ds(c0, w)],
+                mat.at[:, pl.ds(to, w)], si, ri, core_dev,
+            )
+            if cond is None:
+                keep.start()
+                give.start()
+                finals.append((None, keep, give, mat, w, ri))
+            else:
+
+                @pl.when(c == cond)
+                def _():
+                    keep.start()
+                    give.start()
+
+                finals.append((cond, keep, give, mat, w, ri))
+
+    def drain_final(item):
+        cond, keep, give, mat, w, ri = item
+        got = mat.at[:, pl.ds(0, w)]
+        if cond is None:
+            keep.wait()
+            give.wait_send()
+            wait_recv(got, ri)
+        else:
+
+            @pl.when(c == cond)
+            def _():
+                keep.wait()
+                give.wait_send()
+
+            @pl.when(c != cond)
+            def _():
+                wait_recv(got, ri)
+
+    def final_event(j):
+        o = claim_slot()
+        dst = outs.at[o, :, pl.ds(0, widths[j])]
+        gather_final(j, dst, gbs[j].at[z, y], True)
+        n0 = len(finals)
+        final_out(j, dst)
+        mine = finals[n0:]
+        del finals[n0:]
+
+        def last():
+            for item in mine:
+                drain_final(item)
+
+        slot_last[o] = last
+
+    s_f0, r_f0 = take_s(), take_r()
+
+    def final0_send():
+        o = claim_slot()
+        dst = outs.at[o, :, pl.ds(0, widths[0])]
+        w = widths[0]
+        gather_final_h(dst, 1 - y)
+        remote(dst, yb0, s_f0, r_f0, y_dev).start()
+        slot_last[o] = lambda: wait_send(dst, s_f0)
+
+    def gather_final_h(dst, h):
+        gather_final(0, dst, gb0.at[z, h], False, h)
+
+    def final0_finish():
+        o = claim_slot()
+        w = widths[0]
+        dst = outs.at[o, :, pl.ds(0, w)]
+        gather_final_h(dst, y)
+        wait_recv(yb0, r_f0)
+        cp = local(yb0, ld.at[0, :, pl.ds(0, w)], l_e)
+        cp.start()
+        cp.wait()
+        add_more(dst, ld.at[0, :, pl.ds(0, w)])
+        n0 = len(finals)
+        final_out(0, dst)
+        mine = finals[n0:]
+        del finals[n0:]
+
+        def last():
+            for item in mine:
+                drain_final(item)
+
+        slot_last[o] = last
+
+    HALF = 2 * ROWS_CHUNK
+
+    def split_sum(product, cr, xr, base_a, base_d):
+        s_c, r_c = take_s(2), take_r(2)
+        s_x, r_x = take_s(NCH), take_r(NCH)
+        l_c = take_l()
+
+        def give(k, _):
+            def tile(n, _):
+                cols = pl.ds(pl.multiple_of(n * 512, 512), 512)
+                v = product(1, k * HALF, n).astype(BF)
+                ring[pl.ds(base_a + 2 * k, 2), :, cols] = v.reshape(2, ROWS_CHUNK, 512)
+                return 0
+
+            lax.fori_loop(0, D // 512, tile, 0)
+            remote(
+                ring.at[pl.ds(base_a + 2 * k, 2)], cr.at[pl.ds(2 * k, 2)], s_c + k, r_c + k, core_dev
+            ).start()
+            return 0
+
+        lax.fori_loop(0, 2, give, 0)
+
+        def keep(k, _):
+            src = cr.at[pl.ds(2 * k, 2)]
+            wait_recv(src, r_c + k)
+            cp = local(src, rb, l_c)
+            cp.start()
+            cp.wait()
+
+            def tile(n, _):
+                cols = pl.ds(pl.multiple_of(n * 512, 512), 512)
+                v = product(0, k * HALF, n) + rb[:, :, cols].reshape(HALF, 512).astype(F32)
+                ring[pl.ds(base_d + 2 * k, 2), :, cols] = v.astype(BF).reshape(2, ROWS_CHUNK, 512)
+                return 0
+
+            lax.fori_loop(0, D // 512, tile, 0)
+            for i in range(2):
+                remote(
+                    ring.at[base_d + 2 * k + i], xr.at[2 * k + i], s_x + 2 * k + i, r_x + 2 * k + i, x_dev
+                ).start()
+            return 0
+
+        lax.fori_loop(0, 2, keep, 0)
+        for k in range(2):
+            wait_send(ring.at[pl.ds(base_a + 2 * k, 2)], s_c + k)
+        return s_x, r_x
+
+    def rows_at(ref, slot, r0):
+        return ref[slot, pl.ds(pl.multiple_of(r0, HALF), HALF), :]
+
+    def dh_product(slot, r0, n):
+        cols = pl.ds(pl.multiple_of(n * 512, 512), 512)
+        return nt(rows_at(dg, slot, r0), wg_v[cols, :]) + nt(rows_at(du, slot, r0), wu_v[cols, :])
+
+    def dn_product(slot, r0, n):
+        cols = pl.ds(pl.multiple_of(n * 512, 512), 512)
+        return nn(rows_at(hid, slot, r0), wd_v[:, cols])
+
+    s_xdh, r_xdh = split_sum(dh_product, cr_dh, xr_dh, 0, 4)
+    for h in range(2):
+        line_event(0, 0, h)
+    s_xdn, r_xdn = split_sum(dn_product, cr_dn, xr_dn, 0, 8)
+    for cp in load_w_in():
+        cp.start()
+    ld_wout.start()
+
+    for j in (1, 2):
+        line_event(j, 0)
+    for h in range(2):
+        line_event(0, 1, h)
+    line_event(3, 0)
+
+    l_x = take_l()
+    s_do, r_do = take_s(NCH), take_r(NCH)
+    xbuf = rb.at[0]
+
+    def ffn_norm_back(k, _):
+        rows = pl.ds(pl.multiple_of(k * ROWS_CHUNK, ROWS_CHUNK), ROWS_CHUNK)
+        wait_recv(xr_dh.at[k], r_xdh + k)
+        cp = local(xr_dh.at[k], xbuf, l_x)
+        cp.start()
+        cp.wait()
+        d_h = ring[4 + k].astype(F32) + xbuf[...].astype(F32)
+        res = resid[rows, :]
+        s2 = inv_rms(res)
+        n2 = res * s2
+        sm[0, 1:2, :] += jnp.sum(d_h * n2, axis=0, keepdims=True)
+        e2 = d_h * gain_ffn[...]
+        d_res = dy_v[0, rows, :].astype(F32) + s2 * (
+            e2 - n2 * jnp.mean(e2 * n2, axis=-1, keepdims=True)
+        )
+        h2_v[0, rows, :] = d_res.astype(BF)
+        remote(h2_v.at[0, rows], h2_v.at[1, rows], s_do + k, r_do + k, core_dev).start()
+        return 0
+
+    lax.fori_loop(0, NCH, ffn_norm_back, 0)
+    for k in range(NCH):
+        wait_send(ring.at[4 + k], s_xdh + k)
+
+    for cp in load_w_in():
+        cp.wait()
+    ld_wout.wait()
+    for q in range(S):
+
+        def conv_back(j, _, q=q):
+            cols = pl.ds(pl.multiple_of(j * 256, 256), 256)
+            rows = pl.ds(q * T, T)
+            now, one, two = conv_terms(q, cols)
+            k0, k1, k2 = tap_cols(cols)
+            cv = k0 * two + k1 * one + k2 * now
+            d_g = nt(h2_v[0, q * T : q * T + T, :], wd_v[cols, :])
+            d_cv = d_g * pc[rows, cols].astype(F32)
+            sm[0, 2:3, cols] += jnp.sum(d_cv * two, axis=0, keepdims=True)
+            sm[0, 3:4, cols] += jnp.sum(d_cv * one, axis=0, keepdims=True)
+            sm[0, 4:5, cols] += jnp.sum(d_cv * now, axis=0, keepdims=True)
+            after1 = jnp.where(row_iota < T - 1, pltpu.roll(d_cv, T - 1, 0), 0.0)
+            after2 = jnp.where(row_iota < T - 2, pltpu.roll(d_cv, T - 2, 0), 0.0)
+            d_bx = k2 * d_cv + k1 * after1 + k0 * after2
+            dhalo_s[q, :, cols] = d_cv[0:8]
+            tail[q, :, cols] = d_bx[T - 16 : T]
+            old_b = pb[rows, cols]
+            old_x = px[rows, cols]
+            pb_tail[q, :, cols] = old_b[T - 16 : T]
+            px_tail[q, :, cols] = old_x[T - 16 : T]
+            low = d_bx.astype(BF).astype(F32)
+            pb[rows, cols] = (low * old_x.astype(F32)).astype(BF)
+            px[rows, cols] = (low * old_b.astype(F32)).astype(BF)
+            pc[rows, cols] = (d_g * cv).astype(BF)
+            return 0
+
+        lax.fori_loop(0, NC, conv_back, 0)
+
+    s_dha, r_dha = take_s(), take_r()
+    send_dhalo = remote(dhalo_s, dhalo_r, s_dha, r_dha, prev_dev)
+
+    @pl.when(has_prev)
+    def _():
+        send_dhalo.start()
+
+    @pl.when(has_next)
+    def _():
+        wait_recv(dhalo_r, r_dha)
+
+    @pl.when(jnp.logical_not(has_next))
+    def _():
+        dhalo_r[...] = jnp.zeros_like(dhalo_r)
+
+    tail_iota = lax.broadcasted_iota(jnp.int32, (16, CL), 0)
+    for q in range(S):
+        first = jnp.broadcast_to(dhalo_r[q, 0:1, :], (16, CL))
+        second = jnp.broadcast_to(dhalo_r[q, 1:2, :], (16, CL))
+        fix = jnp.where(
+            tail_iota == 14,
+            k_taps[0] * first,
+            jnp.where(tail_iota == 15, k_taps[1] * first + k_taps[0] * second, 0.0),
+        )
+        low = (tail[q] + fix).astype(BF).astype(F32)
+        rows = pl.ds(q * T + T - 16, 16)
+        pb[rows, :] = (low * px_tail[q].astype(F32)).astype(BF)
+        px[rows, :] = (low * pb_tail[q].astype(F32)).astype(BF)
+
+    s_dp, r_dp = take_s(4), take_r(4)
+    theirs = pl.ds(pl.multiple_of((1 - c) * CH, LANE), CH)
+    ours = pl.ds(pl.multiple_of(c * CH, LANE), CH)
+    dp_sends = [
+        remote(ref.at[:, theirs], dy_v.at[1, :, pl.ds(m * CH, CH)], s_dp + m, r_dp + m, core_dev)
+        for m, ref in enumerate((pb, pc, px, gated))
+    ]
+    for cp in dp_sends:
+        cp.start()
+
+    s_x1, r_x1 = take_s(NCH), take_r(NCH)
+
+    def d1_half(k, _):
+        r0 = pl.ds(pl.multiple_of(k * HALF, HALF), HALF)
+
+        def tile(n, _):
+            cols = pl.ds(pl.multiple_of(n * 512, 512), 512)
+            v = (
+                nt(pb[r0, :], wg_v[cols, 0:CL])
+                + nt(pc[r0, :], wg_v[cols, CL : 2 * CL])
+                + nt(px[r0, :], wu_v[cols, 0:CL])
+            )
+            ring[pl.ds(4 + 2 * k, 2), :, cols] = v.astype(BF).reshape(2, ROWS_CHUNK, 512)
+            return 0
+
+        lax.fori_loop(0, D // 512, tile, 0)
+        for i in range(2):
+            remote(
+                ring.at[4 + 2 * k + i], xr_d1.at[2 * k + i], s_x1 + 2 * k + i, r_x1 + 2 * k + i, x_dev
+            ).start()
+        return 0
+
+    lax.fori_loop(0, 2, d1_half, 0)
+
+    wait_recv(h1_v.at[1], r_h1)
+    for k in range(NCH):
+        rows = pl.ds(k * ROWS_CHUNK, ROWS_CHUNK)
+        wait_recv(h2_v.at[1, rows], r_do + k)
+    for m in range(4):
+        wait_recv(dy_v.at[1, :, pl.ds(m * CH, CH)], r_dp + m)
+    W4 = widths[4]
+    g4 = [dg.at[i, pl.ds(k * SR, SR), pl.ds(0, W4)] for i in range(2) for k in range(2)]
+
+    def g_mixer(u, _):
+        zp = order_dyn(u)
+        zc = pl.ds(pl.multiple_of(zp * GR, GR), GR)
+        for m, (mine, lhs) in enumerate(((pb, h1_v), (pc, h1_v), (px, h1_v), (gated, h2_v))):
+            v = tn(lhs[0, :, zc], mine[:, ours]) + tn(
+                lhs[1, :, zc], dy_v[1, :, m * CH : (m + 1) * CH]
+            )
+            v = v.astype(BF)
+            g4[0][:, m * CH : (m + 1) * CH] = v[:SR]
+            g4[1][:, m * CH : (m + 1) * CH] = v[SR:]
+        cps = [local(g4[h], gb4.at[zp, h], l_g + h) for h in range(2)]
+        for cp in cps:
+            cp.start()
+        for cp in cps:
+            cp.wait()
+        remote(gb4.at[zp, 1 - y], yb4.at[zp], s_y[4] + u, r_y[4] + u, y_dev).start()
+        return 0
+
+    lax.fori_loop(0, NZ, g_mixer, 0)
+
+    for h in range(2):
+        line_event(0, 2, h)
+    for e in (1, 2):
+        for j in (1, 2, 3):
+            line_event(j, e)
+    final0_send()
+
+    l_o = take_l()
+
+    def block_chunk(k, _):
+        rows = pl.ds(pl.multiple_of(k * ROWS_CHUNK, ROWS_CHUNK), ROWS_CHUNK)
+        wait_recv(xr_dn.at[k], r_xdn + k)
+        cp = local(xr_dn.at[k], xbuf, l_x)
+        cp.start()
+        cp.wait()
+        total = ring[8 + k].astype(F32) + xbuf[...].astype(F32)
+        rb[1] = (resid[rows, :] + total).astype(BF)
+        co = local(rb.at[1], block_out.at[rows, :], l_o)
+        co.start()
+        co.wait()
+        return 0
+
+    lax.fori_loop(0, NCH, block_chunk, 0)
+    final0_finish()
+
+    def mix_norm_back(k, _):
+        rows = pl.ds(pl.multiple_of(k * ROWS_CHUNK, ROWS_CHUNK), ROWS_CHUNK)
+        wait_recv(xr_d1.at[k], r_x1 + k)
+        cp = local(xr_d1.at[k], xbuf, l_x)
+        cp.start()
+        cp.wait()
+        d_h = ring[4 + k].astype(F32) + xbuf[...].astype(F32)
+        xv = tok_v[rows, :].astype(F32)
+        s1 = inv_rms(xv)
+        n1 = xv * s1
+        sm[0, 0:1, :] += jnp.sum(d_h * n1, axis=0, keepdims=True)
+        e1 = d_h * gain_mix[...]
+        out = h2_v[0, rows, :].astype(F32) + s1 * (
+            e1 - n1 * jnp.mean(e1 * n1, axis=-1, keepdims=True)
+        )
+        rb[1] = out.astype(BF)
+        co = local(rb.at[1], d_tokens.at[rows, :], l_o)
+        co.start()
+        co.wait()
+        return 0
+
+    lax.fori_loop(0, NCH, mix_norm_back, 0)
+
+    for e in range(NZ - 1):
+        line_event(4, e)
+
+    s_sm, r_sm = take_s(2 + NZ), take_r(2 + NZ)
+    a = remote(sm.at[0], sm_r.at[0], s_sm, r_sm, core_dev)
+    a.start()
+    a.wait()
+    sm[1] = sm[0] + sm_r[0]
+    b = remote(sm.at[1], sm_r.at[1], s_sm + 1, r_sm + 1, y_dev)
+    b.start()
+    b.wait()
+    sm[2] = sm[1] + sm_r[1]
+    for k in range(1, NZ):
+        remote(
+            sm.at[2], sm_r.at[1 + k], s_sm + 1 + k, r_sm + 1 + k, did((z + k) % NZ, y, c)
+        ).start()
+    total = sm[2]
+    for k in range(1, NZ):
+        wait_recv(sm_r.at[1 + k], r_sm + 1 + k)
+        total = total + sm_r[1 + k]
+    small_out[...] = total
+    for k in range(1, NZ):
+        wait_send(sm.at[2], s_sm + 1 + k)
+
+    for j in (1, 2, 3, 4):
+        final_event(j)
+
+    for o in range(len(slot_last)):
+        if slot_last[o] is not None:
+            slot_last[o]()
+
+    @pl.when(end)
+    def _():
+        for e in range(NZ - 1):
+            for h in range(2):
+                wait_send(gb0.at[0, h], s_z[0] + 2 * e + h)
+
+    for j in range(1, 5):
+        for u in range(NZ):
+            wait_send(ybs[j].at[0], s_y[j] + u)
+    send_h1.wait_send()
+    for k in range(NCH):
+        wait_send(h2_v.at[0, pl.ds(k * ROWS_CHUNK, ROWS_CHUNK)], s_do + k)
+        wait_send(ring.at[4 + k], s_x1 + k)
+        wait_send(ring.at[8 + k], s_xdn + k)
+    for cp in dp_sends:
+        cp.wait_send()
+
+    @pl.when(has_next)
+    def _():
+        send_halo.wait_send()
+
+    @pl.when(has_prev)
+    def _():
+        send_dhalo.wait_send()
+
+
+def fused_body(tokens, gain_mix, w_in, kernel, w_out, gain_ffn, w_gate, w_up, w_down, cotangent):
+    S, T, D = tokens.shape
+    CL = w_out.shape[0]
+    FL = w_gate.shape[1]
+    R = S * T
+    n_seq = lax.axis_size("seq")
+    tiles = FL // LANE
+    FW = -(-tiles // 2) * LANE
+    GR = D // NZ
+    SR = GR // 2
+    DR = SR // 2
+    widths = [ZF_COLS, FW - ZF_COLS, FW, FW, 2 * CL]
+    NCH = R // ROWS_CHUNK
+
+    def sds(shape, dtype=BF):
+        return jax.ShapeDtypeStruct(shape, dtype)
+
+    outs = [sds((R, D)), sds((R, D)), sds((3, DR, FL)), sds((4, DR, CL)), sds((8, D), F32)]
+    outs += [sds((NZ, 2, SR, w)) for w in widths]
+    outs += [sds((SR, widths[0]))] + [sds((NZ, SR, w)) for w in widths[1:]]
+    outs += [sds((2, NZ, 2, SR, widths[0]))] + [sds((2, NZ, SR, w)) for w in widths[1:]]
+    outs += [sds((NCH, ROWS_CHUNK, D))] * 5
+    any_spec = pl.BlockSpec(memory_space=pl.ANY)
+    vmem_spec = pl.BlockSpec(memory_space=pltpu.VMEM)
+    V = pltpu.VMEM
+    scratch = [
+        V((R, D), BF),
+        V((D, FW), BF),
+        V((D, FW), BF),
+        V((FW, D), BF),
+        V((2, R, D), BF),
+        V((2, R, D), BF),
+        V((2, R, D), BF),
+        V((2, R, FW), BF),
+        V((2, R, FW), BF),
+        V((2, R, FW), BF),
+        V((R, CL), BF),
+        V((R, CL), BF),
+        V((R, CL), BF),
+        V((R, CL), BF),
+        V((R, CL), BF),
+        V((R, D), F32),
+        V((NCH, ROWS_CHUNK, D), BF),
+        V((12, ROWS_CHUNK, D), BF),
+        V((2, ROWS_CHUNK, D), BF),
+        V((4, SR, FW), BF),
+        V((4, SR, FW), BF),
+        V((S, 16, CL), BF),
+        V((S, 16, CL), BF),
+        V((S, 8, CL), F32),
+        V((S, 8, CL), F32),
+        V((S, 16, CL), F32),
+        V((S, 16, CL), BF),
+        V((S, 16, CL), BF),
+        V((3, 8, D), F32),
+        V((1 + NZ, 8, D), F32),
+        pltpu.SemaphoreType.DMA((N_SEND,)),
+        pltpu.SemaphoreType.DMA((N_RECV,)),
+        pltpu.SemaphoreType.DMA((N_LOCAL,)),
+    ]
+    flops = 2 * R * D * (4 * CL + 3 * FL) * 3
+    res = pl.pallas_call(
+        functools.partial(step_kernel, (R, T, D, CL, FL, FW)),
+        out_shape=outs,
+        in_specs=[
+            any_spec, vmem_spec, any_spec, vmem_spec, any_spec, vmem_spec,
+            any_spec, any_spec, any_spec, any_spec,
+        ],
+        out_specs=[any_spec] * 4 + [vmem_spec] + [any_spec] * (len(outs) - 5),
+        scratch_shapes=scratch,
+        compiler_params=pltpu.CompilerParams(
+            collective_id=0, has_side_effects=True, vmem_limit_bytes=63 << 20
+        ),
+        cost_estimate=pl.CostEstimate(flops=flops, bytes_accessed=200 << 20, transcendentals=0),
+        name="block_step",
+    )(
+        tokens.reshape(R, D), gain_mix.reshape(1, D), w_in, kernel, w_out,
+        gain_ffn.reshape(1, D), w_gate, w_up, w_down, cotangent.reshape(R, D),
+    )
+    block_out, d_tokens, g_ffn, g_conv, small = res[:5]
+    s = lax.axis_index("seq")
+    per_d, per_c = D // n_seq, CL // n_seq
+    gains = lax.dynamic_slice(small[0:2], (0, s * per_d), (2, per_d))
+    g_taps = lax.dynamic_slice(small[2:5], (0, s * per_c), (3, per_c))
+    return (
+        block_out.reshape(S, T, D),
+        d_tokens.reshape(S, T, D),
+        gains[0],
+        g_conv[0:3].astype(F32),
+        g_taps.reshape(3, 1, per_c),
+        g_conv[3].astype(F32).T,
+        gains[1],
+        g_ffn[1].astype(F32),
+        g_ffn[2].astype(F32),
+        g_ffn[0].astype(F32).T,
+    )
 
 
 def from_behind(value, axis, by):
@@ -37,7 +1083,7 @@
     )
 
 
-def body(tokens, gain_mix, w_in, kernel, w_out, gain_ffn, w_gate, w_up, w_down, cotangent):
+def general_body(tokens, gain_mix, w_in, kernel, w_out, gain_ffn, w_gate, w_up, w_down, cotangent):
     seq_count, tok_rows, model_width = tokens.shape
     row_count = seq_count * tok_rows
     tokens_f = tokens.astype(jnp.float32).reshape(row_count, model_width)
@@ -146,6 +1192,7 @@
 
 
 def solution(mesh):
+    body = fused_body if mesh.shape["seq"] == 4 * NZ else general_body
     placed = (
         P(None, "seq", None),
         P(),

time: 1250 us -> 374 us (0.30)
  waiting for transfers between devices: 981 us -> 0 us
  Pallas kernels: 0 us -> 356 us
  matrix products: 139 us -> 0 us
  blocking collectives: 62.4 us -> 0 us
  other arithmetic: 34.4 us -> 7.26 us
  between operations: 15.3 us -> 0.66 us
    reduce_scatter x5 -> x0, waiting for transfers between devices: 803 us -> none  [the longest x1 217 us: body(): lax.psum_scatter(g_w_down, 'seq', scatter_dimension=1, tiled=True)]
    pallas_call x0 -> x1, Pallas kernels: none -> 356 us  [fused_body(): pl.pallas_call(functools.partial(step_kernel, (R, T, D, CL, FL, FW)), out...]
    psum x3 -> x0, waiting for transfers between devices: 175 us -> none  [the longest x1 78.7 us: body(): lax.psum(matmul(hidden, w_down).astype(jnp.bfloat16), 'chan')]
    dot_general x21 -> x0, matrix products: 139 us -> none  [the longest x7 53.3 us: left_trans(): lax.dot_general(lhs_mat, rhs_mat, (((0,), (0,)), ((), ())), preferred_ele...]
    unnamed x1 -> x0, blocking collectives: 62.4 us -> none
  transfers between devices with their start and end apart: 11 -> 0, of which waited for: 10 -> 0; matrix products, arithmetic and copies ran while one was open for 7% -> 0% of each run, Pallas kernels for 0% -> 0%
where the time goes in v1:
time: 374 us; the launch traced here: 372 us
  Pallas kernels  356 us (95%)
  local copies, waits for them, and re-layouts  8.55 us (2%)
  other arithmetic  7.26 us (2%)
    pallas_call x1, Pallas kernels, fused_body(): pl.pallas_call(functools.partial(step_kernel, (R, T, D, CL, FL, FW)), out...  356 us

profile of v1, /device:TPU:0, one launch (start us, length us, event | category | flops | bytes accessed | tf_op | source)
XLA Modules:
  0.0 372.2 jit_solution(562842601121167575)
XLA Ops:
  0.6 1.3 reshape.50.gain_mix
  1.9 1.3 reshape.51.gain_ffn
  3.2 355.7 %block_step.1 = (bf16[512,1536]{1,0:T(8,128)(2,1)}, bf16[512,1536]{1,0:T(8,128)(2,1)}, bf16[3,96,3456]{2,1,0:T(8,128)(2,1)}, bf16[4,96,768]{2,1,0:T(8,128)(2,1)}...) custom-call(bf16[512,1536]{1,0:T(8,128)(2,1)} %bitcast.26, ...), custom_call_target="tpu_custom_call" | custom-call | flops 63417876480 | bytes 209715200 | tf_op jit(solution)/shard_map/block_step/pallas_call | solution.py:1018
  358.9 0.8 slice.27
  359.7 0.1 constant_dynamic-slice_fusion.1
  359.8 0.5 slice_bitcast_fusion
  360.3 2.0 slice_convert_fusion
  362.3 0.8 slice.30
  363.1 0.1 constant_dynamic-slice_fusion
  363.2 0.6 reshape.55
  363.8 1.6 convert_bitcast_fusion.1
  365.4 0.0 copy-start.1
  365.4 3.6 convert_bitcast_fusion
  369.1 0.0 copy-start
  369.1 0.0 copy-done.1
  369.1 1.1 copy.22
  370.2 0.8 copy-done
  371.0 1.1 copy.23
Async XLA Ops:
  365.4 3.6 copy-start.1
  369.1 2.0 copy-start

commit v2 on v1

--- a/solution.py
+++ b/solution.py
@@ -46,11 +46,30 @@
 
 N_SEND, N_RECV, N_LOCAL = 128, 192, 64
 
+SCHEDULE = {
+    "dhA": (("mid", (0, 0)),),
+    "dhD": (("mid", (0, 2)),),
+    "dnA": (("end", (3, 0)), ("end", (2, 0)),),
+    "dnD": (("mid", (0, 1)),),
+    "nb0": (("end", (1, 0)),),
+    "nb2": (("end", (2, 1)), ("mid", "pair"),),
+    "d1a": (("mid", (2, 0)),),
+    "tail": (("mid", (3, 0)),),
+    "d1b": (("end", (3, 1)), ("mid", (2, 2)),),
+    "gc0": (("mid", (3, 1)), ("mid", (1, 2)),),
+    "gc2": (("end", "pair"), ("mid", "pair sum"),),
+    "blk1": (("mid", (1, 0)), ("mid", (1, 3)),),
+    "blk3": (("mid", (2, 1)), ("mid", (3, 2)), ("mid", (2, 3)),),
+    "dt0": (("end", (1, 1)), ("end", (2, 2)), ("end", (1, 2)), ("end", (3, 2)),),
+    "dt2": (("end", (4, 0)), ("end", (4, 1)), ("mid", (4, 0)), ("mid", (1, 1)), ("mid", (4, 2)), ("mid", (4, 1)),),
+    "sm": (("end", (4, 2)), ("end", (2, 3)), ("end", (3, 3)), ("end", (1, 3)), ("end", "pair sum"), ("end", (4, 3)), ("mid", (3, 3)), ("mid", (4, 3)),),
+}
+
 
 def step_kernel(
     dims,
     tokens, gain_mix, w_in, taps, w_out, gain_ffn, w_gate, w_up, w_down, cot,
-    block_out, d_tokens, g_ffn, g_conv, small_out,
+    block_out, d_tokens, g_ffn, g_conv, g_gain_mix, g_taps, g_gain_ffn,
     gb0, gb1, gb2, gb3, gb4, yb0, yb1, yb2, yb3, yb4, zb0, zb1, zb2, zb3, zb4,
     cr_dh, cr_dn, xr_dh, xr_dn, xr_d1,
     tok_v, wg_v, wu_v, wd_v, dy_v, h2_v, h1_v, hid, dg, du, pb, pc, px, bx, gated, resid, mix_r,
@@ -109,7 +128,6 @@
     ld_wout = local(w_out, wout_view, l_wout)
     ld_wout.start()
     ld_dy = local(cot, dy_v.at[0], l_dy)
-    ld_dy.start()
 
     bar = pltpu.get_barrier_semaphore()
 
@@ -117,119 +135,142 @@
         pl.semaphore_signal(bar, inc=1, device_id=dev, device_id_type=MESH)
 
     greet(core_dev)
-    greet(y_dev)
     greet(x_dev)
-    for k in range(1, NZ):
-        greet(did((z + k) % NZ, y, c))
+    others = [(k, did((z + k // 2) % NZ, (y + k % 2) % 2, c)) for k in range(1, 2 * NZ)]
+    for _, dev in others:
+        greet(dev)
     has_prev = s > 0
     has_next = s < n_seq - 1
     prev_dev = ((s + n_seq - 1) % n_seq, x)
     next_dev = ((s + 1) % n_seq, x)
     greet(prev_dev)
     greet(next_dev)
-    pl.semaphore_wait(bar, 4 + NZ)
-
-    s_dy, r_dy = take_s(), take_r()
-    send_dy = remote(cot, dy_v.at[1], s_dy, r_dy, core_dev)
-    send_dy.start()
-
-    sm[...] = jnp.zeros_like(sm)
-    k_taps = [taps[t : t + 1, :] for t in range(3)]
-
-    ld_tok.wait()
-
-    def norm_rows(k, _):
-        rows = pl.ds(pl.multiple_of(k * ROWS_CHUNK, ROWS_CHUNK), ROWS_CHUNK)
-        xv = tok_v[rows, :].astype(F32)
-        h1_v[0, rows, :] = (xv * inv_rms(xv) * gain_mix[...]).astype(BF)
-        return 0
-
-    lax.fori_loop(0, NCH, norm_rows, 0)
-    s_h1, r_h1 = take_s(), take_r()
-    send_h1 = remote(h1_v.at[0], h1_v.at[1], s_h1, r_h1, core_dev)
-    send_h1.start()
-    for cp in load_w_in():
-        cp.wait()
-
-    NC = CL // 256
-
-    def in_proj(j, _):
-        cols = pl.ds(pl.multiple_of(j * 256, 256), 256)
-        cols1 = pl.ds(pl.multiple_of(CL + j * 256, 256), 256)
-        h = h1_v[0]
-        b = nn(h, wg_v[:, cols])
-        pb[:, cols] = b.astype(BF)
-        xx = nn(h, wu_v[:, cols])
-        px[:, cols] = xx.astype(BF)
-        bx[:, cols] = (b * xx).astype(BF)
-        pc[:, cols] = nn(h, wg_v[:, cols1]).astype(BF)
-        return 0
-
-    lax.fori_loop(0, NC, in_proj, 0)
     l_w = take_l(3)
     win_start = pl.multiple_of(c * (FL - FW), LANE)
     ld_wg = local(w_gate.at[:, pl.ds(win_start, FW)], wg_v, l_w)
     ld_wu = local(w_up.at[:, pl.ds(win_start, FW)], wu_v, l_w + 1)
     ld_wd = local(w_down.at[pl.ds(win_start, FW), :], wd_v, l_w + 2)
-    ld_wg.start()
-    ld_wu.start()
-
-    s_ha, r_ha = take_s(), take_r()
-    for q in range(S):
-        halo_s[q] = bx[q * T + T - 16 : q * T + T, :]
-    send_halo = remote(halo_s, halo_r, s_ha, r_ha, next_dev)
-
-    @pl.when(has_next)
-    def _():
-        send_halo.start()
-
-    @pl.when(has_prev)
-    def _():
-        wait_recv(halo_r, r_ha)
-
-    @pl.when(jnp.logical_not(has_prev))
-    def _():
-        halo_r[...] = jnp.zeros_like(halo_r)
-
+
+    sm[...] = jnp.zeros_like(sm)
+    gain_mix_row = gain_mix[...].reshape(1, D)
+    gain_ffn_row = gain_ffn[...].reshape(1, D)
+    k_taps = [taps[t : t + 1, :] for t in range(3)]
+
+    ld_tok.wait()
+
+    CPS = T // ROWS_CHUNK
+    NC = CL // 256
+    s_h1, r_h1 = take_s(S), take_r(S)
+    s_ha, r_ha = take_s(S), take_r(S)
+    s_mx, r_mx = take_s(NCH), take_r(NCH)
     row_iota = lax.broadcasted_iota(jnp.int32, (T, 256), 0)
-
-    def conv_terms(q, cols):
-        now = bx[pl.ds(q * T, T), cols].astype(F32)
-        h = halo_r[q, :, cols].astype(F32)
+    top_iota = row_iota[0:16]
+
+    def conv_terms(now, h, iota):
         h14 = jnp.broadcast_to(h[14:15], now.shape)
         h15 = jnp.broadcast_to(h[15:16], now.shape)
-        one = jnp.where(row_iota == 0, h15, pltpu.roll(now, 1, 0))
-        two = jnp.where(row_iota == 0, h14, jnp.where(row_iota == 1, h15, pltpu.roll(now, 2, 0)))
+        one = jnp.where(iota == 0, h15, pltpu.roll(now, 1, 0))
+        two = jnp.where(iota == 0, h14, jnp.where(iota == 1, h15, pltpu.roll(now, 2, 0)))
         return now, one, two
 
     def tap_cols(cols):
         return [taps[t : t + 1, cols] for t in range(3)]
 
-    ld_wout.wait()
-    s_mx, r_mx = take_s(NCH), take_r(NCH)
-    CPS = T // ROWS_CHUNK
+    def convolve(terms, cols):
+        now, one, two = terms
+        k0, k1, k2 = tap_cols(cols)
+        return k0 * two + k1 * one + k2 * now
+
+    def h1_send(q):
+        rows = pl.ds(q * T, T)
+        return remote(h1_v.at[0, rows], h1_v.at[1, rows], s_h1 + q, r_h1 + q, core_dev)
+
+    def halo_send(q):
+        return remote(halo_s.at[q], halo_r.at[q], s_ha + q, r_ha + q, next_dev)
+
+    def mixer_out(k):
+        rows = slice(k * ROWS_CHUNK, (k + 1) * ROWS_CHUNK)
+
+        def out_tile(j, _):
+            cols = pl.ds(pl.multiple_of(j * 512, 512), 512)
+            ring[k, :, cols] = nn(gated[rows, :], wd_v[0:CL, cols]).astype(BF)
+            return 0
+
+        lax.fori_loop(0, D // 512, out_tile, 0)
+        remote(ring.at[k], mix_r.at[k], s_mx + k, r_mx + k, x_dev).start()
+
     for q in range(S):
-
-        def conv_tile(j, _, q=q):
+        rows = pl.ds(q * T, T)
+
+        def norm_rows(k, _, q=q):
+            chunk = pl.ds(pl.multiple_of(q * T + k * ROWS_CHUNK, ROWS_CHUNK), ROWS_CHUNK)
+            xv = tok_v[chunk, :].astype(F32)
+            h1_v[0, chunk, :] = (xv * inv_rms(xv) * gain_mix_row).astype(BF)
+            return 0
+
+        lax.fori_loop(0, CPS, norm_rows, 0)
+        if q == 0:
+            for cp in load_w_in():
+                cp.wait()
+
+        def in_proj(j, _, q=q, rows=rows):
             cols = pl.ds(pl.multiple_of(j * 256, 256), 256)
-            now, one, two = conv_terms(q, cols)
-            k0, k1, k2 = tap_cols(cols)
-            cv = k0 * two + k1 * one + k2 * now
-            rows = pl.ds(q * T, T)
-            gated[rows, cols] = (pc[rows, cols].astype(F32) * cv).astype(BF)
+            cols1 = pl.ds(pl.multiple_of(CL + j * 256, 256), 256)
+            h = h1_v[0, rows, :]
+            b = nn(h, wg_v[:, cols])
+            pb[rows, cols] = b.astype(BF)
+            xx = nn(h, wu_v[:, cols])
+            px[rows, cols] = xx.astype(BF)
+            inner = (b * xx).astype(BF)
+            bx[rows, cols] = inner
+            halo_s[q, :, cols] = inner[T - 16 : T]
+            pcv = nn(h, wg_v[:, cols1])
+            pc[rows, cols] = pcv.astype(BF)
+            now = inner.astype(F32)
+            cv = convolve(conv_terms(now, jnp.zeros_like(now[0:16]), row_iota), cols)
+            gated[rows, cols] = (pcv * cv).astype(BF)
             return 0
 
-        lax.fori_loop(0, NC, conv_tile, 0)
-
-        def out_tile(j, _, q=q):
-            cols = pl.ds(pl.multiple_of(j * 512, 512), 512)
-            v = nn(gated[q * T : q * T + T, :], wd_v[0:CL, cols]).astype(BF)
-            ring[q * CPS : q * CPS + CPS, :, cols] = v.reshape(CPS, ROWS_CHUNK, 512)
+        lax.fori_loop(0, NC, in_proj, 0)
+        if q == 0:
+            pl.semaphore_wait(bar, 3 + 2 * NZ)
+        if q == S - 1:
+            ld_wg.start()
+            ld_wu.start()
+
+        @pl.when(has_next)
+        def _(q=q):
+            halo_send(q).start()
+
+        if q == 0:
+            ld_wout.wait()
+        for k in range(CPS - 1, 0, -1):
+            mixer_out(q * CPS + k)
+
+        @pl.when(has_prev)
+        def _(q=q):
+            wait_recv(halo_r.at[q], r_ha + q)
+
+        @pl.when(jnp.logical_not(has_prev))
+        def _(q=q):
+            halo_r[q] = jnp.zeros_like(halo_r[q])
+
+        def conv_top(j, _, q=q):
+            cols = pl.ds(pl.multiple_of(j * 256, 256), 256)
+            top = pl.ds(q * T, 16)
+            now = bx[top, cols].astype(F32)
+            cv = convolve(conv_terms(now, halo_r[q, :, cols].astype(F32), top_iota), cols)
+            gated[top, cols] = (pc[top, cols].astype(F32) * cv).astype(BF)
             return 0
 
-        lax.fori_loop(0, D // 512, out_tile, 0)
-        for k in range(q * CPS, q * CPS + CPS):
-            remote(ring.at[k], mix_r.at[k], s_mx + k, r_mx + k, x_dev).start()
+        lax.fori_loop(0, NC, conv_top, 0)
+        mixer_out(q * CPS)
+        h1_send(q).start()
+        if q == 0:
+            ld_dy.start()
+            s_dy, r_dy = take_s(), take_r()
+            send_dy = remote(cot, dy_v.at[1], s_dy, r_dy, core_dev)
+            send_dy.start()
     ld_wd.start()
 
     s_h2, r_h2 = take_s(NCH), take_r(NCH)
@@ -247,7 +288,7 @@
         wait_recv(mix_r.at[k], r_mx + k)
         res = tok_v[rows, :].astype(F32) + (ring[k].astype(F32) + mix_r[k].astype(F32))
         resid[rows, :] = res
-        h2_v[0, rows, :] = (res * inv_rms(res) * gain_ffn[...]).astype(BF)
+        h2_v[0, rows, :] = (res * inv_rms(res) * gain_ffn_row).astype(BF)
         remote(h2_v.at[0, rows], h2_v.at[1, rows], s_h2 + k, r_h2 + k, core_dev).start()
 
     def ffn_chunk(k):
@@ -273,14 +314,17 @@
 
         lax.fori_loop(0, NF, tile, 0)
 
-    residual_chunk(0)
+    def sent(k):
+        return (k // CPS) * CPS + (CPS - 1 - k % CPS)
+
+    residual_chunk(sent(0))
 
     def chunk_loop(k, _):
         @pl.when(k + 1 < NCH)
         def _():
-            residual_chunk(k + 1)
-
-        ffn_chunk(k)
+            residual_chunk(sent(k + 1))
+
+        ffn_chunk(sent(k))
         return 0
 
     lax.fori_loop(0, NCH, chunk_loop, 0)
@@ -301,7 +345,7 @@
         if e == NZ - 1:
             return z
         per_z = {0: (3, 2, 1), 1: (3, 0, 2), 2: (0, 3, 1), 3: (0, 1, 2)}
-        v = jnp.int32(per_z[3][e])
+        v = per_z[3][e]
         for zz in range(3):
             v = jnp.where(z == zz, per_z[zz][e], v)
         return v
@@ -324,10 +368,14 @@
 
     l_g = take_l(12)
 
-    def g_block(lhs_ref, rhs_ref, zp, pair):
+    def y_send(j, u):
+        zp = order_dyn(u) if not isinstance(u, int) else order(u)
+        return remote(gbs[j].at[zp, 1 - y], ybs[j].at[zp], s_y[j] + u, r_y[j] + u, y_dev)
+
+    def g_block(lhs_ref, rhs_ref, zp, pair, parts=(0, 1)):
         lhs = lhs_ref[:, :, pl.ds(pl.multiple_of(zp * GR, GR), GR)].reshape(2 * R, GR)
         half = FW // 2
-        for n in range(2):
+        for n in parts:
             v = tn(lhs, rhs_ref[:, :, n * half : (n + 1) * half].reshape(2 * R, half)).astype(BF)
             outs[2 * pair, :, n * half : (n + 1) * half] = v[:SR]
             outs[2 * pair + 1, :, n * half : (n + 1) * half] = v[SR:]
@@ -350,47 +398,57 @@
         def plain_copies(gb, pair, li):
             return [local(outs.at[2 * pair + h], gb.at[zp, h], li + h) for h in range(2)]
 
-        def y_send(j):
-            remote(gbs[j].at[zp, 1 - y], ybs[j].at[zp], s_y[j] + u, r_y[j] + u, y_dev).start()
-
         g_block(dy_v, hid, zp, 0)
         for cp in down_copies():
             cp.start()
-        g_block(h2_v, dg, zp, 1)
-        for cp in plain_copies(gb2, 1, l_g + 4):
-            cp.start()
+        g_block(h2_v, dg, zp, 1, (0,))
         for cp in down_copies():
             cp.wait()
-        y_send(1)
+
+        @pl.when(u < 3)
+        def _():
+            y_send(1, u).start()
 
         @pl.when(jnp.logical_and(end, u < NZ - 1))
         def _():
             for h in range(2):
                 z_send(0, gb0.at[zp, h], u, zp, h).start()
 
+        g_block(h2_v, dg, zp, 1, (1,))
+        for cp in plain_copies(gb2, 1, l_g + 4):
+            cp.start()
         g_block(h2_v, du, zp, 0)
         for cp in plain_copies(gb3, 0, l_g + 6):
             cp.start()
         for cp in plain_copies(gb2, 1, l_g + 4):
             cp.wait()
-        y_send(2)
+
+        @pl.when(u < 2)
+        def _():
+            y_send(2, u).start()
+
         for cp in plain_copies(gb3, 0, l_g + 6):
             cp.wait()
-        y_send(3)
+
+        @pl.when(u < 2)
+        def _():
+            y_send(3, u).start()
+
         return 0
 
     lax.fori_loop(0, NZ, g_step, 0)
 
     l_e = take_l(4)
-    slot_last = [None] * outs.shape[0]
-    slot_next = [0]
-
-    def claim_slot():
-        o = slot_next[0]
-        slot_next[0] = (o + 1) % outs.shape[0]
-        if slot_last[o] is not None:
-            slot_last[o]()
-            slot_last[o] = None
+    is_role = {"end": end, "mid": mid}
+    slot_last = {role: [None] * outs.shape[0] for role in is_role}
+    slot_next = {role: 0 for role in is_role}
+
+    def claim_slot(role):
+        o = slot_next[role]
+        slot_next[role] = (o + 1) % outs.shape[0]
+        if slot_last[role][o] is not None:
+            slot_last[role][o]()
+            slot_last[role][o] = None
         return o
 
     ADD_ROWS = 32
@@ -406,228 +464,161 @@
 
         lax.fori_loop(0, SR // ADD_ROWS, rows_add, 0)
 
-    def add_more(dst, src):
-        def rows_add(k, _):
-            rows = pl.ds(pl.multiple_of(k * ADD_ROWS, ADD_ROWS), ADD_ROWS)
-            dst[rows, :] = (dst[rows, :].astype(F32) + src[rows, :].astype(F32)).astype(BF)
-            return 0
-
-        lax.fori_loop(0, SR // ADD_ROWS, rows_add, 0)
-
-    def line_event(j, e, h=None):
-        zp = order(e)
-        w = widths[j]
-        d = jnp.where(zp > z, 0, 1)
-        la, lb, lc = (ld.at[i, :, pl.ds(0, w)] for i in range(3))
+    def fetch(srcs, w):
+        views, copies = [], []
+        for i, (src, ri) in enumerate(srcs):
+            if ri is not None:
+                wait_recv(src, ri)
+            views.append(ld.at[i, :, pl.ds(0, w)])
+            copies.append(local(src, views[-1], l_e + i))
+            copies[-1].start()
+        for cp in copies:
+            cp.wait()
+        return views
+
+    def from_line(j, d, zp, h=None):
         if h is None:
-            zsrc, ri = zbs[j].at[d, zp], r_z[j] + d * NZ + zp
-            si = s_z[j] + e
-            o = claim_slot()
-            dst = outs.at[o, :, pl.ds(0, w)]
-            ca = local(gbs[j].at[zp, y], la, l_e)
-            ca.start()
-            wait_recv(ybs[j].at[zp], r_y[j] + e)
-            cb = local(ybs[j].at[zp], lb, l_e + 1)
-            cb.start()
-
-            @pl.when(mid)
-            def _():
-                wait_recv(zsrc, ri)
-                cc = local(zsrc, lc, l_e + 2)
-                cc.start()
-                ca.wait()
-                cb.wait()
-                cc.wait()
-                add_into(dst, [la, lb, lc])
-
-            @pl.when(end)
-            def _():
-                ca.wait()
-                cb.wait()
-                add_into(dst, [la, lb])
-
-            z_send(j, dst, e, zp).start()
-            slot_last[o] = lambda: wait_send(dst, si)
+            return zbs[j].at[d, zp], r_z[j] + d * NZ + zp
+        return zbs[j].at[d, zp, h], r_z[j] + (d * NZ + zp) * 2 + h
+
+    def line_event(role, j, e):
+        @pl.when(is_role[role])
+        def _():
+            zp = order(e)
+            w = widths[j]
+            d = jnp.where(zp > z, 0, 1)
+            for h in (0, 1) if j == 0 else (None,):
+                o = claim_slot(role)
+                dst = outs.at[o, :, pl.ds(0, w)]
+                if h is None:
+                    srcs = [(gbs[j].at[zp, y], None), (ybs[j].at[zp], r_y[j] + e)]
+                    si = s_z[j] + e
+                else:
+                    srcs = [(gbs[j].at[zp, h], None)]
+                    si = s_z[j] + 2 * e + h
+                if role == "mid":
+                    srcs.append(from_line(j, d, zp, h))
+                add_into(dst, fetch(srcs, w))
+                z_send(j, dst, e, zp, h).start()
+                slot_last[role][o] = functools.partial(sent_slot, o, w, si)
+
+    def sent_slot(o, w, si):
+        wait_send(outs.at[o, :, pl.ds(0, w)], si)
+
+    def own_shard(role, j, h=None):
+        if h is None:
+            srcs = [(gbs[j].at[z, y], None), (ybs[j].at[z], r_y[j] + NZ - 1)]
         else:
-            zsrc, ri = zbs[j].at[d, zp, h], r_z[j] + (d * NZ + zp) * 2 + h
-            si = s_z[j] + 2 * e + h
-            o = claim_slot()
-            dst = outs.at[o, :, pl.ds(0, w)]
-
-            @pl.when(mid)
-            def _():
-                ca = local(gbs[j].at[zp, h], la, l_e)
-                ca.start()
-                wait_recv(zsrc, ri)
-                cc = local(zsrc, lc, l_e + 2)
-                cc.start()
-                ca.wait()
-                cc.wait()
-                add_into(dst, [la, lc])
-                z_send(j, dst, e, zp, h).start()
-
-            def last():
-                @pl.when(mid)
-                def _():
-                    wait_send(dst, si)
-
-            slot_last[o] = last
-
-    def gather_final(j, dst, own, with_y, h=None):
-        w = widths[j]
-        la, lb, lc, ldd = (ld.at[i, :, pl.ds(0, w)] for i in range(4))
-        ca = local(own, la, l_e)
-        ca.start()
-        if with_y:
-            wait_recv(ybs[j].at[z], r_y[j] + NZ - 1)
-            cb = local(ybs[j].at[z], lb, l_e + 1)
-            cb.start()
-
-        def side(d):
-            if h is None:
-                return zbs[j].at[d, z], r_z[j] + d * NZ + z
-            return zbs[j].at[d, z, h], r_z[j] + (d * NZ + z) * 2 + h
-
-        def fetch(d, to, li):
-            src, ri = side(d)
-            wait_recv(src, ri)
-            cp = local(src, to, li)
-            cp.start()
-            return cp
-
-        base = [la, lb] if with_y else [la]
-
-        def finish(cps, srcs):
-            ca.wait()
-            if with_y:
-                cb.wait()
-            for cp in cps:
-                cp.wait()
-            add_into(dst, srcs)
-
-        @pl.when(mid)
-        def _():
-            c0 = fetch(0, lc, l_e + 2)
-            c1 = fetch(1, ldd, l_e + 3)
-            finish([c0, c1], base + [lc, ldd])
-
-        @pl.when(z == 0)
-        def _():
-            c1 = fetch(1, ldd, l_e + 3)
-            finish([c1], base + [ldd])
-
-        @pl.when(z == NZ - 1)
-        def _():
-            c0 = fetch(0, lc, l_e + 2)
-            finish([c0], base + [lc])
-
-    finals = []
-
-    def swap_pieces(j, dst):
+            srcs = [(gbs[j].at[z, h], None)]
+        if role == "mid":
+            return srcs + [from_line(j, 0, z, h), from_line(j, 1, z, h)]
+        return srcs + [from_line(j, jnp.where(z == 0, 1, 0), z, h)]
+
+    def swap_pieces(j):
         if j == 4:
             return [(None, m * CH, CH, g_conv.at[m], c * CH) for m in range(4)]
         mat = g_ffn.at[{0: 0, 1: 0, 2: 1, 3: 2}[j]]
-        off = ZF_COLS if j == 1 else 0
         w = widths[j]
         if j == 1:
-            return [(None, 0, w, mat, c * (FL - FW) + off)]
+            return [(None, 0, w, mat, c * (FL - FW) + ZF_COLS)]
         return [(0, 0, w, mat, 0), (1, overlap, w - overlap, mat, FL - FW + overlap)]
 
-    def final_out(j, dst):
-        for cond, c0, w, mat, to in swap_pieces(j, dst):
-            si, ri, li = take_s(), take_r(), take_l()
-            to = pl.multiple_of(to, LANE) if not isinstance(to, int) else to
-            keep = local(
-                dst.at[pl.ds(pl.multiple_of(c * DR, DR), DR), pl.ds(c0, w)],
-                mat.at[:, pl.ds(to, w)], li,
-            )
-            give = remote(
-                dst.at[pl.ds(pl.multiple_of((1 - c) * DR, DR), DR), pl.ds(c0, w)],
-                mat.at[:, pl.ds(to, w)], si, ri, core_dev,
-            )
-            if cond is None:
+    swap_sems = [[(take_s(), take_r(), take_l()) for _ in swap_pieces(j)] for j in range(5)]
+
+    def swap(j, o):
+        items = []
+        for (core, c0, w, mat, to), (si, ri, li) in zip(swap_pieces(j), swap_sems[j]):
+            to = to if isinstance(to, int) else pl.multiple_of(to, LANE)
+            target = mat.at[:, pl.ds(to, w)]
+            mine = outs.at[o, pl.ds(pl.multiple_of(c * DR, DR), DR), pl.ds(c0, w)]
+            other = outs.at[o, pl.ds(pl.multiple_of((1 - c) * DR, DR), DR), pl.ds(c0, w)]
+            items.append((core, local(mine, target, li), remote(other, target, si, ri, core_dev), target))
+        return items
+
+    def swap_start(j, o):
+        for core, keep, give, _ in swap(j, o):
+            if core is None:
                 keep.start()
                 give.start()
-                finals.append((None, keep, give, mat, w, ri))
             else:
 
-                @pl.when(c == cond)
+                @pl.when(c == core)
                 def _():
                     keep.start()
                     give.start()
 
-                finals.append((cond, keep, give, mat, w, ri))
-
-    def drain_final(item):
-        cond, keep, give, mat, w, ri = item
-        got = mat.at[:, pl.ds(0, w)]
-        if cond is None:
-            keep.wait()
-            give.wait_send()
-            wait_recv(got, ri)
-        else:
-
-            @pl.when(c == cond)
-            def _():
+    def swap_finish(j, o):
+        for (core, keep, give, target), (_, ri, _) in zip(swap(j, o), swap_sems[j]):
+            if core is None:
                 keep.wait()
                 give.wait_send()
-
-            @pl.when(c != cond)
-            def _():
-                wait_recv(got, ri)
-
-    def final_event(j):
-        o = claim_slot()
-        dst = outs.at[o, :, pl.ds(0, widths[j])]
-        gather_final(j, dst, gbs[j].at[z, y], True)
-        n0 = len(finals)
-        final_out(j, dst)
-        mine = finals[n0:]
-        del finals[n0:]
-
-        def last():
-            for item in mine:
-                drain_final(item)
-
-        slot_last[o] = last
+                wait_recv(target, ri)
+            else:
+
+                @pl.when(c == core)
+                def _():
+                    keep.wait()
+                    give.wait_send()
+
+                @pl.when(c != core)
+                def _():
+                    wait_recv(target, ri)
+
+    def final_event(role, j):
+        @pl.when(is_role[role])
+        def _():
+            o = claim_slot(role)
+            w = widths[j]
+            add_into(outs.at[o, :, pl.ds(0, w)], fetch(own_shard(role, j), w))
+            swap_start(j, o)
+            slot_last[role][o] = functools.partial(swap_finish, j, o)
 
     s_f0, r_f0 = take_s(), take_r()
-
-    def final0_send():
-        o = claim_slot()
-        dst = outs.at[o, :, pl.ds(0, widths[0])]
-        w = widths[0]
-        gather_final_h(dst, 1 - y)
-        remote(dst, yb0, s_f0, r_f0, y_dev).start()
-        slot_last[o] = lambda: wait_send(dst, s_f0)
-
-    def gather_final_h(dst, h):
-        gather_final(0, dst, gb0.at[z, h], False, h)
-
-    def final0_finish():
-        o = claim_slot()
-        w = widths[0]
-        dst = outs.at[o, :, pl.ds(0, w)]
-        gather_final_h(dst, y)
-        wait_recv(yb0, r_f0)
-        cp = local(yb0, ld.at[0, :, pl.ds(0, w)], l_e)
-        cp.start()
-        cp.wait()
-        add_more(dst, ld.at[0, :, pl.ds(0, w)])
-        n0 = len(finals)
-        final_out(0, dst)
-        mine = finals[n0:]
-        del finals[n0:]
-
-        def last():
-            for item in mine:
-                drain_final(item)
-
-        slot_last[o] = last
+    w0 = widths[0]
+
+    def final0_send(role):
+        @pl.when(is_role[role])
+        def _():
+            o = claim_slot(role)
+            dst = outs.at[o, :, pl.ds(0, w0)]
+            add_into(dst, fetch(own_shard(role, 0, 1 - y), w0))
+            cp = local(dst, gb0.at[z, 1 - y], l_e)
+            cp.start()
+            cp.wait()
+            remote(gb0.at[z, 1 - y], yb0, s_f0, r_f0, y_dev).start()
+
+    def final0_finish(role):
+        @pl.when(is_role[role])
+        def _():
+            o = claim_slot(role)
+            dst = outs.at[o, :, pl.ds(0, w0)]
+            add_into(dst, fetch(own_shard(role, 0, y), w0))
+            add_into(dst, [dst] + fetch([(yb0, r_f0)], w0))
+            swap_start(0, o)
+            slot_last[role][o] = functools.partial(swap_finish, 0, o)
+
+    def hook(name):
+        for role, event in SCHEDULE.get(name, ()):
+            if event == "pair":
+                final0_send(role)
+            elif event == "pair sum":
+                final0_finish(role)
+            elif event[1] == NZ - 1:
+                final_event(role, event[0])
+            else:
+                line_event(role, *event)
+
+    def chunks(name, count, body):
+        first = 0
+        for k in range(count):
+            if SCHEDULE.get(name + str(k)) or k == count - 1:
+                lax.fori_loop(first, k + 1, body, 0)
+                first = k + 1
+                hook(name + str(k))
 
     HALF = 2 * ROWS_CHUNK
 
-    def split_sum(product, cr, xr, base_a, base_d):
+    def split_sum(name, product, cr, xr, base_a, base_d):
         s_c, r_c = take_s(2), take_r(2)
         s_x, r_x = take_s(NCH), take_r(NCH)
         l_c = take_l()
@@ -646,6 +637,7 @@
             return 0
 
         lax.fori_loop(0, 2, give, 0)
+        hook(name + "A")
 
         def keep(k, _):
             src = cr.at[pl.ds(2 * k, 2)]
@@ -670,6 +662,7 @@
         lax.fori_loop(0, 2, keep, 0)
         for k in range(2):
             wait_send(ring.at[pl.ds(base_a + 2 * k, 2)], s_c + k)
+        hook(name + "D")
         return s_x, r_x
 
     def rows_at(ref, slot, r0):
@@ -683,19 +676,11 @@
         cols = pl.ds(pl.multiple_of(n * 512, 512), 512)
         return nn(rows_at(hid, slot, r0), wd_v[:, cols])
 
-    s_xdh, r_xdh = split_sum(dh_product, cr_dh, xr_dh, 0, 4)
-    for h in range(2):
-        line_event(0, 0, h)
-    s_xdn, r_xdn = split_sum(dn_product, cr_dn, xr_dn, 0, 8)
+    s_xdh, r_xdh = split_sum("dh", dh_product, cr_dh, xr_dh, 0, 4)
+    s_xdn, r_xdn = split_sum("dn", dn_product, cr_dn, xr_dn, 0, 8)
     for cp in load_w_in():
         cp.start()
     ld_wout.start()
-
-    for j in (1, 2):
-        line_event(j, 0)
-    for h in range(2):
-        line_event(0, 1, h)
-    line_event(3, 0)
 
     l_x = take_l()
     s_do, r_do = take_s(NCH), take_r(NCH)
@@ -712,7 +697,7 @@
         s2 = inv_rms(res)
         n2 = res * s2
         sm[0, 1:2, :] += jnp.sum(d_h * n2, axis=0, keepdims=True)
-        e2 = d_h * gain_ffn[...]
+        e2 = d_h * gain_ffn_row
         d_res = dy_v[0, rows, :].astype(F32) + s2 * (
             e2 - n2 * jnp.mean(e2 * n2, axis=-1, keepdims=True)
         )
@@ -720,7 +705,7 @@
         remote(h2_v.at[0, rows], h2_v.at[1, rows], s_do + k, r_do + k, core_dev).start()
         return 0
 
-    lax.fori_loop(0, NCH, ffn_norm_back, 0)
+    chunks("nb", NCH, ffn_norm_back)
     for k in range(NCH):
         wait_send(ring.at[4 + k], s_xdh + k)
 
@@ -732,7 +717,9 @@
         def conv_back(j, _, q=q):
             cols = pl.ds(pl.multiple_of(j * 256, 256), 256)
             rows = pl.ds(q * T, T)
-            now, one, two = conv_terms(q, cols)
+            now, one, two = conv_terms(
+                bx[rows, cols].astype(F32), halo_r[q, :, cols].astype(F32), row_iota
+            )
             k0, k1, k2 = tap_cols(cols)
             cv = k0 * two + k1 * one + k2 * now
             d_g = nt(h2_v[0, q * T : q * T + T, :], wd_v[cols, :])
@@ -764,6 +751,38 @@
     def _():
         send_dhalo.start()
 
+    for j, u in ((2, 2), (3, 2), (1, 3), (2, 3), (3, 3)):
+        y_send(j, u).start()
+
+    hook("cb")
+
+    s_x1, r_x1 = take_s(NCH), take_r(NCH)
+
+    def d1_part(name, ids):
+        def tile(n, _):
+            cols = pl.ds(pl.multiple_of(n * 512, 512), 512)
+
+            def rows_of(ref):
+                return jnp.concatenate(
+                    [ref[k * ROWS_CHUNK : (k + 1) * ROWS_CHUNK, :] for k in ids], axis=0
+                )
+
+            v = (
+                nt(rows_of(pb), wg_v[cols, 0:CL])
+                + nt(rows_of(pc), wg_v[cols, CL : 2 * CL])
+                + nt(rows_of(px), wu_v[cols, 0:CL])
+            ).astype(BF)
+            for i, k in enumerate(ids):
+                ring[4 + k, :, cols] = v[i * ROWS_CHUNK : (i + 1) * ROWS_CHUNK]
+            return 0
+
+        lax.fori_loop(0, D // 512, tile, 0)
+        for k in ids:
+            remote(ring.at[4 + k], xr_d1.at[k], s_x1 + k, r_x1 + k, x_dev).start()
+        hook(name)
+
+    d1_part("d1a", [q * CPS + k for q in range(S) for k in range(CPS - 1)])
+
     @pl.when(has_next)
     def _():
         wait_recv(dhalo_r, r_dha)
@@ -795,32 +814,12 @@
     ]
     for cp in dp_sends:
         cp.start()
-
-    s_x1, r_x1 = take_s(NCH), take_r(NCH)
-
-    def d1_half(k, _):
-        r0 = pl.ds(pl.multiple_of(k * HALF, HALF), HALF)
-
-        def tile(n, _):
-            cols = pl.ds(pl.multiple_of(n * 512, 512), 512)
-            v = (
-                nt(pb[r0, :], wg_v[cols, 0:CL])
-                + nt(pc[r0, :], wg_v[cols, CL : 2 * CL])
-                + nt(px[r0, :], wu_v[cols, 0:CL])
-            )
-            ring[pl.ds(4 + 2 * k, 2), :, cols] = v.astype(BF).reshape(2, ROWS_CHUNK, 512)
-            return 0
-
-        lax.fori_loop(0, D // 512, tile, 0)
-        for i in range(2):
-            remote(
-                ring.at[4 + 2 * k + i], xr_d1.at[2 * k + i], s_x1 + 2 * k + i, r_x1 + 2 * k + i, x_dev
-            ).start()
-        return 0
-
-    lax.fori_loop(0, 2, d1_half, 0)
-
-    wait_recv(h1_v.at[1], r_h1)
+    hook("tail")
+
+    d1_part("d1b", [q * CPS + k for q in range(S) for k in range(1, CPS)])
+
+    for q in range(S):
+        wait_recv(h1_v.at[1, pl.ds(q * T, T)], r_h1 + q)
     for k in range(NCH):
         rows = pl.ds(k * ROWS_CHUNK, ROWS_CHUNK)
         wait_recv(h2_v.at[1, rows], r_do + k)
@@ -844,17 +843,10 @@
             cp.start()
         for cp in cps:
             cp.wait()
-        remote(gb4.at[zp, 1 - y], yb4.at[zp], s_y[4] + u, r_y[4] + u, y_dev).start()
+        y_send(4, u).start()
         return 0
 
-    lax.fori_loop(0, NZ, g_mixer, 0)
-
-    for h in range(2):
-        line_event(0, 2, h)
-    for e in (1, 2):
-        for j in (1, 2, 3):
-            line_event(j, e)
-    final0_send()
+    chunks("gc", NZ, g_mixer)
 
     l_o = take_l()
 
@@ -871,10 +863,10 @@
         co.wait()
         return 0
 
-    lax.fori_loop(0, NCH, block_chunk, 0)
-    final0_finish()
-
-    def mix_norm_back(k, _):
+    chunks("blk", NCH, block_chunk)
+
+    def mix_norm_back(n, _):
+        k = (n % S) * CPS + n // S
         rows = pl.ds(pl.multiple_of(k * ROWS_CHUNK, ROWS_CHUNK), ROWS_CHUNK)
         wait_recv(xr_d1.at[k], r_x1 + k)
         cp = local(xr_d1.at[k], xbuf, l_x)
@@ -885,7 +877,7 @@
         s1 = inv_rms(xv)
         n1 = xv * s1
         sm[0, 0:1, :] += jnp.sum(d_h * n1, axis=0, keepdims=True)
-        e1 = d_h * gain_mix[...]
+        e1 = d_h * gain_mix_row
         out = h2_v[0, rows, :].astype(F32) + s1 * (
             e1 - n1 * jnp.mean(e1 * n1, axis=-1, keepdims=True)
         )
@@ -895,38 +887,38 @@
         co.wait()
         return 0
 
-    lax.fori_loop(0, NCH, mix_norm_back, 0)
-
-    for e in range(NZ - 1):
-        line_event(4, e)
-
-    s_sm, r_sm = take_s(2 + NZ), take_r(2 + NZ)
+    chunks("dt", NCH, mix_norm_back)
+
+    s_sm, r_sm = take_s(2 * NZ), take_r(2 * NZ)
     a = remote(sm.at[0], sm_r.at[0], s_sm, r_sm, core_dev)
     a.start()
     a.wait()
     sm[1] = sm[0] + sm_r[0]
-    b = remote(sm.at[1], sm_r.at[1], s_sm + 1, r_sm + 1, y_dev)
-    b.start()
-    b.wait()
-    sm[2] = sm[1] + sm_r[1]
-    for k in range(1, NZ):
-        remote(
-            sm.at[2], sm_r.at[1 + k], s_sm + 1 + k, r_sm + 1 + k, did((z + k) % NZ, y, c)
-        ).start()
-    total = sm[2]
-    for k in range(1, NZ):
-        wait_recv(sm_r.at[1 + k], r_sm + 1 + k)
-        total = total + sm_r[1 + k]
-    small_out[...] = total
-    for k in range(1, NZ):
-        wait_send(sm.at[2], s_sm + 1 + k)
-
-    for j in (1, 2, 3, 4):
-        final_event(j)
-
-    for o in range(len(slot_last)):
-        if slot_last[o] is not None:
-            slot_last[o]()
+    for k, dev in others:
+        remote(sm.at[1], sm_r.at[k], s_sm + k, r_sm + k, dev).start()
+    hook("sm")
+
+    total = sm[1]
+    for k, _ in others:
+        wait_recv(sm_r.at[k], r_sm + k)
+        total = total + sm_r[k]
+    for k, _ in others:
+        wait_send(sm.at[1], s_sm + k)
+    per_d, per_c = D // n_seq, CL // n_seq
+    mine = pltpu.roll(total, D - s * per_d, 1)
+    g_gain_mix[...] = mine[0, 0:per_d]
+    g_gain_ffn[...] = mine[1, 0:per_d]
+    mine = pltpu.roll(total, D - s * per_c, 1)
+    for t in range(3):
+        g_taps[t] = mine[2 + t : 3 + t, 0:per_c]
+
+    for role, cond in is_role.items():
+
+        @pl.when(cond)
+        def _(role=role):
+            for finish in slot_last[role]:
+                if finish is not None:
+                    finish()
 
     @pl.when(end)
     def _():
@@ -937,7 +929,9 @@
     for j in range(1, 5):
         for u in range(NZ):
             wait_send(ybs[j].at[0], s_y[j] + u)
-    send_h1.wait_send()
+    wait_send(yb0, s_f0)
+    for q in range(S):
+        h1_send(q).wait_send()
     for k in range(NCH):
         wait_send(h2_v.at[0, pl.ds(k * ROWS_CHUNK, ROWS_CHUNK)], s_do + k)
         wait_send(ring.at[4 + k], s_x1 + k)
@@ -947,7 +941,8 @@
 
     @pl.when(has_next)
     def _():
-        send_halo.wait_send()
+        for q in range(S):
+            halo_send(q).wait_send()
 
     @pl.when(has_prev)
     def _():
@@ -971,7 +966,8 @@
     def sds(shape, dtype=BF):
         return jax.ShapeDtypeStruct(shape, dtype)
 
-    outs = [sds((R, D)), sds((R, D)), sds((3, DR, FL)), sds((4, DR, CL)), sds((8, D), F32)]
+    outs = [sds((R, D)), sds((R, D)), sds((3, DR, FL)), sds((4, DR, CL))]
+    outs += [sds((D // n_seq,), F32), sds((3, 1, CL // n_seq), F32), sds((D // n_seq,), F32)]
     outs += [sds((NZ, 2, SR, w)) for w in widths]
     outs += [sds((SR, widths[0]))] + [sds((NZ, SR, w)) for w in widths[1:]]
     outs += [sds((2, NZ, 2, SR, widths[0]))] + [sds((2, NZ, SR, w)) for w in widths[1:]]
@@ -1008,8 +1004,8 @@
         V((S, 16, CL), F32),
         V((S, 16, CL), BF),
         V((S, 16, CL), BF),
-        V((3, 8, D), F32),
-        V((1 + NZ, 8, D), F32),
+        V((2, 8, D), F32),
+        V((2 * NZ, 8, D), F32),
         pltpu.SemaphoreType.DMA((N_SEND,)),
         pltpu.SemaphoreType.DMA((N_RECV,)),
         pltpu.SemaphoreType.DMA((N_LOCAL,)),
@@ -1022,7 +1018,7 @@
             any_spec, vmem_spec, any_spec, vmem_spec, any_spec, vmem_spec,
             any_spec, any_spec, any_spec, any_spec,
         ],
-        out_specs=[any_spec] * 4 + [vmem_spec] + [any_spec] * (len(outs) - 5),
+        out_specs=[any_spec] * 4 + [vmem_spec] * 3 + [any_spec] * (len(outs) - 7),
         scratch_shapes=scratch,
         compiler_params=pltpu.CompilerParams(
             collective_id=0, has_side_effects=True, vmem_limit_bytes=63 << 20
@@ -1030,22 +1026,18 @@
         cost_estimate=pl.CostEstimate(flops=flops, bytes_accessed=200 << 20, transcendentals=0),
         name="block_step",
     )(
-        tokens.reshape(R, D), gain_mix.reshape(1, D), w_in, kernel, w_out,
-        gain_ffn.reshape(1, D), w_gate, w_up, w_down, cotangent.reshape(R, D),
-    )
-    block_out, d_tokens, g_ffn, g_conv, small = res[:5]
-    s = lax.axis_index("seq")
-    per_d, per_c = D // n_seq, CL // n_seq
-    gains = lax.dynamic_slice(small[0:2], (0, s * per_d), (2, per_d))
-    g_taps = lax.dynamic_slice(small[2:5], (0, s * per_c), (3, per_c))
+        tokens.reshape(R, D), gain_mix, w_in, kernel, w_out,
+        gain_ffn, w_gate, w_up, w_down, cotangent.reshape(R, D),
+    )
+    block_out, d_tokens, g_ffn, g_conv, g_gain_mix, g_taps, g_gain_ffn = res[:7]
     return (
         block_out.reshape(S, T, D),
         d_tokens.reshape(S, T, D),
-        gains[0],
+        g_gain_mix,
         g_conv[0:3].astype(F32),
-        g_taps.reshape(3, 1, per_c),
+        g_taps,
         g_conv[3].astype(F32).T,
-        gains[1],
+        g_gain_ffn,
         g_ffn[1].astype(F32),
         g_ffn[2].astype(F32),
         g_ffn[0].astype(F32).T,

time: 374 us -> 291 us (0.78)
  Pallas kernels: 356 us -> 277 us
  local copies, waits for them, and re-layouts: 8.55 us -> 4.71 us
    pallas_call x1, Pallas kernels: 356 us -> 277 us  [fused_body(): pl.pallas_call(functools.partial(step_kernel, (R, T, D, CL, FL, FW)), out...]
where the time goes in v2:
time: 291 us; the launch traced here: 289 us
  Pallas kernels  277 us (95%)
  other arithmetic  7.27 us (2%)
  local copies, waits for them, and re-layouts  4.71 us (2%)
    pallas_call x1, Pallas kernels, fused_body(): pl.pallas_call(functools.partial(step_kernel, (R, T, D, CL, FL, FW)), out...  277 us

profile of v2, /device:TPU:0, one launch (start us, length us, event | category | flops | bytes accessed | tf_op | source)
XLA Modules:
  0.0 289.3 jit_solution(924712744242108852)
XLA Ops:
  0.6 276.7 %block_step.1 = (bf16[512,1536]{1,0:T(8,128)(2,1)}, bf16[512,1536]{1,0:T(8,128)(2,1)}, bf16[3,96,3456]{2,1,0:T(8,128)(2,1)}, bf16[4,96,768]{2,1,0:T(8,128)(2,1)}...) custom-call(bf16[512,1536]{1,0:T(8,128)(2,1)} %bitcast.22, ...), custom_call_target="tpu_custom_call" | custom-call | flops 63417876480 | bytes 209715200 | tf_op jit(solution)/shard_map/block_step/pallas_call | solution.py:1014
  277.3 1.6 convert_bitcast_fusion.1
  279.0 2.0 slice_convert_fusion
  281.0 0.0 copy-start.1
  281.0 3.6 %convert_bitcast_fusion = (f32[3456,96]{0,1:T(8,128)}, f32[96,3456]{1,0:T(8,128)}, f32[96,3456]{1,0:T(8,128)}) fusion(bf16[3,96,3456]{2,1,0:T(8,128)(2,1)} %get-tuple-element.23), kind=kLoop, calls=%fused_computation | loop fusion | flops 995328 | bytes 5971968 | tf_op jit(solution)/shard_map/transpose | solution.py:1043
  284.6 0.0 copy-start
  284.6 0.0 copy-done.1
  284.6 1.1 copy.25
  285.8 0.8 copy-done
  286.6 0.0 copy-start.4
  286.6 0.0 copy-start.2
  286.6 0.0 copy-start.3
  286.6 1.1 copy.26
  287.7 0.0 copy-done.4
  287.7 0.5 copy.27
  288.3 0.0 copy-done.2
  288.3 0.6 copy.28
  288.8 0.0 copy-done.3
  288.8 0.5 copy.29
Async XLA Ops:
  281.0 3.6 %copy-start.1 = (bf16[512,1536]{1,0:T(8,128)(2,1)S(1)}, bf16[512,1536]{1,0:T(8,128)(2,1)}, u32[]{:S(2)}) copy-start(bf16[512,1536]{1,0:T(8,128)(2,1)} %get-tuple-element.17) | copy-start | bytes 4718596
  284.6 2.0 copy-start
  286.6 1.2 copy-start.4
  286.6 1.7 copy-start.2
  286.6 2.2 copy-start.3

commit v3 on v2

--- a/solution.py
+++ b/solution.py
@@ -47,32 +47,33 @@
 N_SEND, N_RECV, N_LOCAL = 128, 192, 64
 
 SCHEDULE = {
-    "dhA": (("mid", (0, 0)),),
-    "dhD": (("mid", (0, 2)),),
-    "dnA": (("end", (3, 0)), ("end", (2, 0)),),
-    "dnD": (("mid", (0, 1)),),
-    "nb0": (("end", (1, 0)),),
-    "nb2": (("end", (2, 1)), ("mid", "pair"),),
-    "d1a": (("mid", (2, 0)),),
-    "tail": (("mid", (3, 0)),),
-    "d1b": (("end", (3, 1)), ("mid", (2, 2)),),
-    "gc0": (("mid", (3, 1)), ("mid", (1, 2)),),
-    "gc2": (("end", "pair"), ("mid", "pair sum"),),
-    "blk1": (("mid", (1, 0)), ("mid", (1, 3)),),
-    "blk3": (("mid", (2, 1)), ("mid", (3, 2)), ("mid", (2, 3)),),
-    "dt0": (("end", (1, 1)), ("end", (2, 2)), ("end", (1, 2)), ("end", (3, 2)),),
-    "dt2": (("end", (4, 0)), ("end", (4, 1)), ("mid", (4, 0)), ("mid", (1, 1)), ("mid", (4, 2)), ("mid", (4, 1)),),
-    "sm": (("end", (4, 2)), ("end", (2, 3)), ("end", (3, 3)), ("end", (1, 3)), ("end", "pair sum"), ("end", (4, 3)), ("mid", (3, 3)), ("mid", (4, 3)),),
+    "dhA": (("end", (1, 1)), ("mid", (0, 0)),),
+    "dhD": (("mid", (0, 2)), ("mid", (0, 1)),),
+    "dnD": (("end", (2, 0)),),
+    "nb1": (("end", "pair"), ("end", (2, 1)), ("mid", "pair"),),
+    "cb": (("mid", (2, 0)),),
+    "d1a": (("end", (3, 0)),),
+    "tail": (("mid", (1, 2)),),
+    "d1b": (("end", (1, 0)), ("end", (1, 2)), ("end", (3, 1)),),
+    "gc0": (("mid", (3, 0)),),
+    "gc1": (("end", (3, 2)),),
+    "blk1": (("end", (4, 0)), ("end", (2, 2)),),
+    "blk2": (("end", "pair sum"), ("end", (4, 1)), ("end", (4, 2)), ("end", (1, 3)),),
+    "blk3": (("mid", (1, 0)), ("mid", (2, 2)),),
+    "dt0": (("mid", (3, 1)),),
+    "dt2": (("mid", (2, 1)), ("mid", (3, 2)), ("mid", (1, 1)), ("mid", (4, 0)), ("mid", "pair sum"),),
+    "dt3": (("end", (3, 3)), ("mid", (2, 3)), ("mid", (4, 1)),),
+    "sm": (("end", (2, 3)), ("end", (4, 3)), ("mid", (1, 3)), ("mid", (4, 2)), ("mid", (3, 3)), ("mid", (4, 3)),),
 }
 
 
 def step_kernel(
     dims,
-    tokens, gain_mix, w_in, taps, w_out, gain_ffn, w_gate, w_up, w_down, cot,
-    block_out, d_tokens, g_ffn, g_conv, g_gain_mix, g_taps, g_gain_ffn,
+    tokens, gain_mix_hbm, w_in, taps_hbm, w_out, gain_ffn_hbm, w_gate, w_up, w_down, cot,
+    block_out, d_tokens, g_ffn, g_conv, small_out,
     gb0, gb1, gb2, gb3, gb4, yb0, yb1, yb2, yb3, yb4, zb0, zb1, zb2, zb3, zb4,
     cr_dh, cr_dn, xr_dh, xr_dn, xr_d1,
-    tok_v, wg_v, wu_v, wd_v, dy_v, h2_v, h1_v, hid, dg, du, pb, pc, px, bx, gated, resid, mix_r,
+    gain_mix, taps, gain_ffn, tok_v, wg_v, wu_v, wd_v, dy_v, h2_v, h1_v, hid, dg, du, pb, pc, px, bx, gated, resid, mix_r,
     ring, rb, ld, outs, halo_s, halo_r, dhalo_s, dhalo_r, tail, pb_tail, px_tail,
     sm, sm_r, ss, rs, ls,
 ):
@@ -114,7 +115,7 @@
     def local(src, dst, li):
         return pltpu.make_async_copy(src, dst, ls.at[li])
 
-    l_tok, l_win, l_wout, l_dy = take_l(), take_l(3), take_l(), take_l()
+    l_tok, l_win, l_wout, l_dy, l_small = take_l(), take_l(3), take_l(), take_l(), take_l(3)
     ld_tok = local(tokens, tok_v, l_tok)
     ld_tok.start()
     win_views = [wg_v.at[:, pl.ds(0, CL)], wg_v.at[:, pl.ds(CL, CL)], wu_v.at[:, pl.ds(0, CL)]]
@@ -124,6 +125,14 @@
         return [local(w_in.at[m], win_views[m], l_win + m) for m in range(3)]
 
     for cp in load_w_in():
+        cp.start()
+    ld_small = [
+        local(src, dst, l_small + i)
+        for i, (src, dst) in enumerate(
+            ((gain_mix_hbm, gain_mix), (taps_hbm, taps), (gain_ffn_hbm, gain_ffn))
+        )
+    ]
+    for cp in ld_small:
         cp.start()
     ld_wout = local(w_out, wout_view, l_wout)
     ld_wout.start()
@@ -152,6 +161,8 @@
     ld_wd = local(w_down.at[pl.ds(win_start, FW), :], wd_v, l_w + 2)
 
     sm[...] = jnp.zeros_like(sm)
+    for cp in ld_small:
+        cp.wait()
     gain_mix_row = gain_mix[...].reshape(1, D)
     gain_ffn_row = gain_ffn[...].reshape(1, D)
     k_taps = [taps[t : t + 1, :] for t in range(3)]
@@ -274,60 +285,43 @@
     ld_wd.start()
 
     s_h2, r_h2 = take_s(NCH), take_r(NCH)
-    ld_dy.wait()
-    send_dy.wait()
     ld_wg.wait()
     ld_wu.wait()
-    ld_wd.wait()
     NF = FW // 256
     overlap = 2 * FW - FL
     col_iota = lax.broadcasted_iota(jnp.int32, (2 * ROWS_CHUNK, 256), 1)
 
-    def residual_chunk(k):
+    def forward_chunk(n, _):
+        k = (n // CPS) * CPS + (CPS - 1 - n % CPS)
         rows = pl.ds(pl.multiple_of(k * ROWS_CHUNK, ROWS_CHUNK), ROWS_CHUNK)
         wait_recv(mix_r.at[k], r_mx + k)
         res = tok_v[rows, :].astype(F32) + (ring[k].astype(F32) + mix_r[k].astype(F32))
         resid[rows, :] = res
         h2_v[0, rows, :] = (res * inv_rms(res) * gain_ffn_row).astype(BF)
         remote(h2_v.at[0, rows], h2_v.at[1, rows], s_h2 + k, r_h2 + k, core_dev).start()
-
-    def ffn_chunk(k):
-        rows = pl.ds(pl.multiple_of(k * ROWS_CHUNK, ROWS_CHUNK), ROWS_CHUNK)
         wait_recv(h2_v.at[1, rows], r_h2 + k)
 
         def tile(j, _):
             cols = pl.ds(pl.multiple_of(j * 256, 256), 256)
             h = h2_v[:, rows, :].reshape(2 * ROWS_CHUNK, D)
-            e = dy_v[:, rows, :].reshape(2 * ROWS_CHUNK, D)
             g = nn(h, wg_v[:, cols])
             u = nn(h, wu_v[:, cols])
-            dh = nt(e, wd_v[cols, :])
             keep = col_iota + j * 256 >= c * overlap
             sg = jax.nn.sigmoid(g)
-            si = g * sg
-            dh = jnp.where(keep, dh, 0.0)
+            si = jnp.where(keep, g * sg, 0.0)
             shape = (2, ROWS_CHUNK, 256)
-            hid[:, rows, cols] = jnp.where(keep, si * u, 0.0).astype(BF).reshape(shape)
-            dg[:, rows, cols] = (dh * u * sg * (1.0 + g * (1.0 - sg))).astype(BF).reshape(shape)
-            du[:, rows, cols] = (dh * si).astype(BF).reshape(shape)
+            hid[:, rows, cols] = (si * u).astype(BF).reshape(shape)
+            slope = jnp.where(keep, u * sg * (1.0 + g * (1.0 - sg)), 0.0)
+            dg[:, rows, cols] = slope.astype(BF).reshape(shape)
+            du[:, rows, cols] = si.astype(BF).reshape(shape)
             return 0
 
         lax.fori_loop(0, NF, tile, 0)
-
-    def sent(k):
-        return (k // CPS) * CPS + (CPS - 1 - k % CPS)
-
-    residual_chunk(sent(0))
-
-    def chunk_loop(k, _):
-        @pl.when(k + 1 < NCH)
-        def _():
-            residual_chunk(sent(k + 1))
-
-        ffn_chunk(sent(k))
         return 0
 
-    lax.fori_loop(0, NCH, chunk_loop, 0)
+    lax.fori_loop(0, NCH, forward_chunk, 0)
+    ld_dy.wait()
+    send_dy.wait()
     for k in range(NCH):
         wait_send(ring.at[k], s_mx + k)
         wait_send(h2_v.at[0, pl.ds(k * ROWS_CHUNK, ROWS_CHUNK)], s_h2 + k)
@@ -356,21 +350,35 @@
             v = jnp.where(u == e, order(e), v)
         return v
 
+    def per_core(j, act):
+        if j in (1, 4):
+            act(lambda ref: ref)
+            return
+
+        @pl.when(c == 0)
+        def _():
+            act(lambda ref: ref)
+
+        @pl.when(c == 1)
+        def _():
+            act(lambda ref: ref.at[:, pl.ds(overlap, widths[j] - overlap)])
+
     def z_send(j, src, e, zp, h=None):
         to_right = zp > z
         d = jnp.where(to_right, 0, 1)
         dev = did(jnp.clip(jnp.where(to_right, z + 1, z - 1), 0, NZ - 1), y, c)
         if h is None:
-            return remote(src, zbs[j].at[d, zp], s_z[j] + e, r_z[j] + d * NZ + zp, dev)
-        return remote(
-            src, zbs[j].at[d, zp, h], s_z[j] + 2 * e + h, r_z[j] + (d * NZ + zp) * 2 + h, dev
-        )
+            dst, si, ri = zbs[j].at[d, zp], s_z[j] + e, r_z[j] + d * NZ + zp
+        else:
+            dst, si, ri = zbs[j].at[d, zp, h], s_z[j] + 2 * e + h, r_z[j] + (d * NZ + zp) * 2 + h
+        per_core(j, lambda cut: remote(cut(src), cut(dst), si, ri, dev).start())
 
     l_g = take_l(12)
 
     def y_send(j, u):
         zp = order_dyn(u) if not isinstance(u, int) else order(u)
-        return remote(gbs[j].at[zp, 1 - y], ybs[j].at[zp], s_y[j] + u, r_y[j] + u, y_dev)
+        src, dst = gbs[j].at[zp, 1 - y], ybs[j].at[zp]
+        per_core(j, lambda cut: remote(cut(src), cut(dst), s_y[j] + u, r_y[j] + u, y_dev).start())
 
     def g_block(lhs_ref, rhs_ref, zp, pair, parts=(0, 1)):
         lhs = lhs_ref[:, :, pl.ds(pl.multiple_of(zp * GR, GR), GR)].reshape(2 * R, GR)
@@ -380,63 +388,92 @@
             outs[2 * pair, :, n * half : (n + 1) * half] = v[:SR]
             outs[2 * pair + 1, :, n * half : (n + 1) * half] = v[SR:]
 
-    def g_step(u, _):
+    def down_copies(zp, pair):
+        return [
+            cp
+            for h in range(2)
+            for cp in (
+                local(outs.at[2 * pair + h, :, pl.ds(0, ZF_COLS)], gb0.at[zp, h], l_g + 4 * pair + 2 * h),
+                local(
+                    outs.at[2 * pair + h, :, pl.ds(ZF_COLS, FW - ZF_COLS)],
+                    gb1.at[zp, h], l_g + 4 * pair + 2 * h + 1,
+                ),
+            )
+        ]
+
+    def down_sends(u):
+        zp = order(u)
+        for cp in down_copies(zp, u % 2):
+            cp.wait()
+        if u < NZ - 1:
+
+            @pl.when(end)
+            def _():
+                for h in range(2):
+                    z_send(0, gb0.at[zp, h], u, zp, h)
+
+            y_send(1, u)
+
+    for u in range(NZ):
+        g_block(dy_v, hid, order(u), u % 2, (0,))
+        if u > 0:
+            down_sends(u - 1)
+        g_block(dy_v, hid, order(u), u % 2, (1,))
+        for cp in down_copies(order(u), u % 2):
+            cp.start()
+    down_sends(NZ - 1)
+
+    ld_wd.wait()
+
+    def hid_back(n, _):
+        slot, j = n // NF, n % NF
+        cols = pl.ds(pl.multiple_of(j * 256, 256), 256)
+        dh = nt(dy_v[slot], wd_v[cols, :])
+        dg[slot, :, cols] = (dh * dg[slot, :, cols].astype(F32)).astype(BF)
+        du[slot, :, cols] = (dh * du[slot, :, cols].astype(F32)).astype(BF)
+        return 0
+
+    lax.fori_loop(0, 2 * NF, hid_back, 0)
+
+    def plain_copies(gb, zp, pair):
+        return [local(outs.at[2 * pair + h], gb.at[zp, h], l_g + 2 * pair + h) for h in range(2)]
+
+    def gate_up(u, _):
         zp = order_dyn(u)
 
-        def down_copies():
-            return [
-                cp
-                for h in range(2)
-                for cp in (
-                    local(outs.at[h, :, pl.ds(0, ZF_COLS)], gb0.at[zp, h], l_g + 2 * h),
-                    local(
-                        outs.at[h, :, pl.ds(ZF_COLS, FW - ZF_COLS)], gb1.at[zp, h], l_g + 2 * h + 1
-                    ),
-                )
-            ]
-
-        def plain_copies(gb, pair, li):
-            return [local(outs.at[2 * pair + h], gb.at[zp, h], li + h) for h in range(2)]
-
-        g_block(dy_v, hid, zp, 0)
-        for cp in down_copies():
+        def up_sends(u):
+            for cp in plain_copies(gb3, order_dyn(u), 1):
+                cp.wait()
+
+            @pl.when(u < 2)
+            def _():
+                y_send(3, u)
+
+        g_block(h2_v, dg, zp, 0, (0,))
+
+        @pl.when(u > 0)
+        def _():
+            up_sends(u - 1)
+
+        g_block(h2_v, dg, zp, 0, (1,))
+        for cp in plain_copies(gb2, zp, 0):
             cp.start()
-        g_block(h2_v, dg, zp, 1, (0,))
-        for cp in down_copies():
-            cp.wait()
-
-        @pl.when(u < 3)
-        def _():
-            y_send(1, u).start()
-
-        @pl.when(jnp.logical_and(end, u < NZ - 1))
-        def _():
-            for h in range(2):
-                z_send(0, gb0.at[zp, h], u, zp, h).start()
-
-        g_block(h2_v, dg, zp, 1, (1,))
-        for cp in plain_copies(gb2, 1, l_g + 4):
-            cp.start()
-        g_block(h2_v, du, zp, 0)
-        for cp in plain_copies(gb3, 0, l_g + 6):
-            cp.start()
-        for cp in plain_copies(gb2, 1, l_g + 4):
+        g_block(h2_v, du, zp, 1, (0,))
+        for cp in plain_copies(gb2, zp, 0):
             cp.wait()
 
         @pl.when(u < 2)
         def _():
-            y_send(2, u).start()
-
-        for cp in plain_copies(gb3, 0, l_g + 6):
-            cp.wait()
-
-        @pl.when(u < 2)
-        def _():
-            y_send(3, u).start()
-
+            y_send(2, u)
+
+        g_block(h2_v, du, zp, 1, (1,))
+        for cp in plain_copies(gb3, zp, 1):
+            cp.start()
         return 0
 
-    lax.fori_loop(0, NZ, g_step, 0)
+    lax.fori_loop(0, NZ, gate_up, 0)
+    for cp in plain_copies(gb3, order(NZ - 1), 1):
+        cp.wait()
 
     l_e = take_l(4)
     is_role = {"end": end, "mid": mid}
@@ -464,11 +501,12 @@
 
         lax.fori_loop(0, SR // ADD_ROWS, rows_add, 0)
 
-    def fetch(srcs, w):
+    def fetch(j, srcs):
+        w = widths[j]
         views, copies = [], []
         for i, (src, ri) in enumerate(srcs):
             if ri is not None:
-                wait_recv(src, ri)
+                per_core(j, lambda cut: wait_recv(cut(src), ri))
             views.append(ld.at[i, :, pl.ds(0, w)])
             copies.append(local(src, views[-1], l_e + i))
             copies[-1].start()
@@ -498,12 +536,12 @@
                     si = s_z[j] + 2 * e + h
                 if role == "mid":
                     srcs.append(from_line(j, d, zp, h))
-                add_into(dst, fetch(srcs, w))
-                z_send(j, dst, e, zp, h).start()
-                slot_last[role][o] = functools.partial(sent_slot, o, w, si)
-
-    def sent_slot(o, w, si):
-        wait_send(outs.at[o, :, pl.ds(0, w)], si)
+                add_into(dst, fetch(j, srcs))
+                z_send(j, dst, e, zp, h)
+                slot_last[role][o] = functools.partial(sent_slot, j, o, si)
+
+    def sent_slot(j, o, si):
+        per_core(j, lambda cut: wait_send(cut(outs.at[o, :, pl.ds(0, widths[j])]), si))
 
     def own_shard(role, j, h=None):
         if h is None:
@@ -569,7 +607,7 @@
         def _():
             o = claim_slot(role)
             w = widths[j]
-            add_into(outs.at[o, :, pl.ds(0, w)], fetch(own_shard(role, j), w))
+            add_into(outs.at[o, :, pl.ds(0, w)], fetch(j, own_shard(role, j)))
             swap_start(j, o)
             slot_last[role][o] = functools.partial(swap_finish, j, o)
 
@@ -581,19 +619,20 @@
         def _():
             o = claim_slot(role)
             dst = outs.at[o, :, pl.ds(0, w0)]
-            add_into(dst, fetch(own_shard(role, 0, 1 - y), w0))
+            add_into(dst, fetch(0, own_shard(role, 0, 1 - y)))
             cp = local(dst, gb0.at[z, 1 - y], l_e)
             cp.start()
             cp.wait()
-            remote(gb0.at[z, 1 - y], yb0, s_f0, r_f0, y_dev).start()
+            src = gb0.at[z, 1 - y]
+            per_core(0, lambda cut: remote(cut(src), cut(yb0), s_f0, r_f0, y_dev).start())
 
     def final0_finish(role):
         @pl.when(is_role[role])
         def _():
             o = claim_slot(role)
             dst = outs.at[o, :, pl.ds(0, w0)]
-            add_into(dst, fetch(own_shard(role, 0, y), w0))
-            add_into(dst, [dst] + fetch([(yb0, r_f0)], w0))
+            add_into(dst, fetch(0, own_shard(role, 0, y)))
+            add_into(dst, [dst] + fetch(0, [(yb0, r_f0)]))
             swap_start(0, o)
             slot_last[role][o] = functools.partial(swap_finish, 0, o)
 
@@ -751,8 +790,8 @@
     def _():
         send_dhalo.start()
 
-    for j, u in ((2, 2), (3, 2), (1, 3), (2, 3), (3, 3)):
-        y_send(j, u).start()
+    for j, u in ((2, 2), (3, 2)):
+        y_send(j, u)
 
     hook("cb")
 
@@ -843,10 +882,16 @@
             cp.start()
         for cp in cps:
             cp.wait()
-        y_send(4, u).start()
+
+        @pl.when(u < NZ - 1)
+        def _():
+            y_send(4, u)
+
         return 0
 
     chunks("gc", NZ, g_mixer)
+    for j in (1, 2, 3, 4):
+        y_send(j, NZ - 1)
 
     l_o = take_l()
 
@@ -904,13 +949,10 @@
         total = total + sm_r[k]
     for k, _ in others:
         wait_send(sm.at[1], s_sm + k)
-    per_d, per_c = D // n_seq, CL // n_seq
-    mine = pltpu.roll(total, D - s * per_d, 1)
-    g_gain_mix[...] = mine[0, 0:per_d]
-    g_gain_ffn[...] = mine[1, 0:per_d]
-    mine = pltpu.roll(total, D - s * per_c, 1)
-    for t in range(3):
-        g_taps[t] = mine[2 + t : 3 + t, 0:per_c]
+    sm[0] = total
+    out_small = local(sm.at[0], small_out, l_small)
+    out_small.start()
+    out_small.wait()
 
     for role, cond in is_role.items():
 
@@ -924,12 +966,12 @@
     def _():
         for e in range(NZ - 1):
             for h in range(2):
-                wait_send(gb0.at[0, h], s_z[0] + 2 * e + h)
+                per_core(0, lambda cut: wait_send(cut(gb0.at[0, h]), s_z[0] + 2 * e + h))
 
     for j in range(1, 5):
         for u in range(NZ):
-            wait_send(ybs[j].at[0], s_y[j] + u)
-    wait_send(yb0, s_f0)
+            per_core(j, lambda cut: wait_send(cut(ybs[j].at[0]), s_y[j] + u))
+    per_core(0, lambda cut: wait_send(cut(yb0), s_f0))
     for q in range(S):
         h1_send(q).wait_send()
     for k in range(NCH):
@@ -966,16 +1008,17 @@
     def sds(shape, dtype=BF):
         return jax.ShapeDtypeStruct(shape, dtype)
 
-    outs = [sds((R, D)), sds((R, D)), sds((3, DR, FL)), sds((4, DR, CL))]
-    outs += [sds((D // n_seq,), F32), sds((3, 1, CL // n_seq), F32), sds((D // n_seq,), F32)]
+    outs = [sds((R, D)), sds((R, D)), sds((3, DR, FL)), sds((4, DR, CL)), sds((8, D), F32)]
     outs += [sds((NZ, 2, SR, w)) for w in widths]
     outs += [sds((SR, widths[0]))] + [sds((NZ, SR, w)) for w in widths[1:]]
     outs += [sds((2, NZ, 2, SR, widths[0]))] + [sds((2, NZ, SR, w)) for w in widths[1:]]
     outs += [sds((NCH, ROWS_CHUNK, D))] * 5
     any_spec = pl.BlockSpec(memory_space=pl.ANY)
-    vmem_spec = pl.BlockSpec(memory_space=pltpu.VMEM)
     V = pltpu.VMEM
     scratch = [
+        V((D,), F32),
+        V((3, CL), F32),
+        V((D,), F32),
         V((R, D), BF),
         V((D, FW), BF),
         V((D, FW), BF),
@@ -1014,11 +1057,8 @@
     res = pl.pallas_call(
         functools.partial(step_kernel, (R, T, D, CL, FL, FW)),
         out_shape=outs,
-        in_specs=[
-            any_spec, vmem_spec, any_spec, vmem_spec, any_spec, vmem_spec,
-            any_spec, any_spec, any_spec, any_spec,
-        ],
-        out_specs=[any_spec] * 4 + [vmem_spec] * 3 + [any_spec] * (len(outs) - 7),
+        in_specs=[any_spec] * 10,
+        out_specs=[any_spec] * len(outs),
         scratch_shapes=scratch,
         compiler_params=pltpu.CompilerParams(
             collective_id=0, has_side_effects=True, vmem_limit_bytes=63 << 20
@@ -1029,19 +1069,90 @@
         tokens.reshape(R, D), gain_mix, w_in, kernel, w_out,
         gain_ffn, w_gate, w_up, w_down, cotangent.reshape(R, D),
     )
-    block_out, d_tokens, g_ffn, g_conv, g_gain_mix, g_taps, g_gain_ffn = res[:7]
+    block_out, d_tokens, g_mix, g_in, g_taps, g_out, g_gain, g_gate, g_up, g_down = finish(
+        n_seq, *res[:5]
+    )
     return (
         block_out.reshape(S, T, D),
         d_tokens.reshape(S, T, D),
-        g_gain_mix,
-        g_conv[0:3].astype(F32),
-        g_taps,
-        g_conv[3].astype(F32).T,
-        g_gain_ffn,
-        g_ffn[1].astype(F32),
-        g_ffn[2].astype(F32),
-        g_ffn[0].astype(F32).T,
-    )
+        g_mix, g_in, g_taps, g_out.T, g_gain, g_gate, g_up, g_down.T,
+    )
+
+
+def finish_kernel(
+    n_seq, block_in, d_in, ffn_in, conv_in, small_in,
+    block_out, d_out, g_mix, g_in, g_taps, g_out, g_gain, g_gate, g_up, g_down,
+    block_v, d_v, ffn, conv, small, gate_v, up_v, down_v, in_v, out_v, mix_v, taps_v, gain_v, sem,
+):
+    D = d_in.shape[1]
+    CL = conv_in.shape[2]
+    s = lax.axis_index("seq")
+    count = [0]
+
+    def copy(src, dst):
+        count[0] += 1
+        cp = pltpu.make_async_copy(src, dst, sem.at[count[0] - 1])
+        cp.start()
+        return cp
+
+    loads = [copy(ffn_in.at[0], ffn.at[0]), copy(conv_in, conv), copy(small_in, small)]
+    loads += [copy(ffn_in.at[m], ffn.at[m]) for m in (1, 2)]
+    passing = [copy(block_in, block_v), copy(d_in, d_v)]
+    stores = []
+    loads[0].wait()
+    down_v[...] = ffn[0].astype(F32)
+    stores.append(copy(down_v, g_down))
+    loads[1].wait()
+    in_v[...] = conv[0:3].astype(F32)
+    stores.append(copy(in_v, g_in))
+    out_v[...] = conv[3].astype(F32)
+    stores.append(copy(out_v, g_out))
+    passing[0].wait()
+    stores.append(copy(block_v, block_out))
+    passing[1].wait()
+    stores.append(copy(d_v, d_out))
+    loads[3].wait()
+    gate_v[...] = ffn[1].astype(F32)
+    stores.append(copy(gate_v, g_gate))
+    loads[4].wait()
+    up_v[...] = ffn[2].astype(F32)
+    stores.append(copy(up_v, g_up))
+    loads[2].wait()
+    per_d, per_c = D // n_seq, CL // n_seq
+    mine = pltpu.roll(small[...], D - s * per_d, 1)
+    mix_v[...] = mine[0, 0:per_d]
+    gain_v[...] = mine[1, 0:per_d]
+    mine = pltpu.roll(small[...], D - s * per_c, 1)
+    for t in range(3):
+        taps_v[t] = mine[2 + t : 3 + t, 0:per_c]
+    stores += [copy(mix_v, g_mix), copy(gain_v, g_gain), copy(taps_v, g_taps)]
+    for cp in stores:
+        cp.wait()
+
+
+def finish(n_seq, block_out, d_tokens, g_ffn, g_conv, small):
+    R, D = block_out.shape
+    _, DR, FL = g_ffn.shape
+    CL = g_conv.shape[2]
+    any_spec = pl.BlockSpec(memory_space=pl.ANY)
+    V = pltpu.VMEM
+    tails = [
+        (DR, FL), (DR, FL), (DR, FL), (3, DR, CL), (DR, CL),
+        (D // n_seq,), (3, 1, CL // n_seq), (D // n_seq,),
+    ]
+    gate, up, down, inp, out, mix, taps, gain = [jax.ShapeDtypeStruct(t, F32) for t in tails]
+    low = jax.ShapeDtypeStruct((R, D), BF)
+    return pl.pallas_call(
+        functools.partial(finish_kernel, n_seq),
+        out_shape=[low, low, mix, inp, taps, out, gain, gate, up, down],
+        in_specs=[any_spec] * 5,
+        out_specs=[any_spec] * 10,
+        scratch_shapes=[V((R, D), BF), V((R, D), BF), V(g_ffn.shape, BF), V(g_conv.shape, BF), V(small.shape, F32)]
+        + [V(t, F32) for t in tails]
+        + [pltpu.SemaphoreType.DMA((20,))],
+        compiler_params=pltpu.CompilerParams(vmem_limit_bytes=63 << 20),
+        name="finish",
+    )(block_out, d_tokens, g_ffn, g_conv, small)
 
 
 def from_behind(value, axis, by):

time: 291 us -> 278 us (0.955); the launches traced: 289 us -> 273 us
  other arithmetic: 7.27 us -> 0 us
  Pallas kernels: 277 us -> 272 us
  local copies, waits for them, and re-layouts: 4.71 us -> 0 us
    pallas_call x1, Pallas kernels: 277 us -> 266 us  [fused_body(): pl.pallas_call(functools.partial(step_kernel, (R, T, D, CL, FL, FW)), out...]
    pallas_call x0 -> x1, Pallas kernels: none -> 6.22 us  [finish(): pl.pallas_call(functools.partial(finish_kernel, n_seq), out_shape=[low, l...]
    transpose x2 -> x0, other arithmetic: 5.27 us -> none  [the longest x1 3.63 us: fused_body(): g_ffn[0].astype(F32)]
    unnamed x15 -> x0, local copies, waits for them, and re-layouts: 4.71 us -> none
where the time goes in v3:
time: 278 us; the launch traced here: 273 us
  Pallas kernels  272 us (98%)
    pallas_call x1, Pallas kernels, fused_body(): pl.pallas_call(functools.partial(step_kernel, (R, T, D, CL, FL, FW)), out...  266 us
    pallas_call x1, Pallas kernels, finish(): pl.pallas_call(functools.partial(finish_kernel, n_seq), out_shape=[low, l...  6.22 us

profile of v3, /device:TPU:0, one launch (start us, length us, event | category | flops | bytes accessed | tf_op | source)
XLA Modules:
  0.0 272.6 jit_solution(10330649923256568444)
XLA Ops:
  0.6 265.5 %block_step.1 = (bf16[512,1536]{1,0:T(8,128)(2,1)}, bf16[512,1536]{1,0:T(8,128)(2,1)}, bf16[3,96,3456]{2,1,0:T(8,128)(2,1)}, bf16[4,96,768]{2,1,0:T(8,128)(2,1)}...) custom-call(bf16[512,1536]{1,0:T(8,128)(2,1)} %bitcast.6, ...), custom_call_target="tpu_custom_call" | custom-call | flops 63417876480 | bytes 209715200 | tf_op jit(solution)/shard_map/block_step/pallas_call | solution.py:1057
  266.2 6.2 %finish.1 = (bf16[512,1536]{1,0:T(8,128)(2,1)}, bf16[512,1536]{1,0:T(8,128)(2,1)}, f32[96]{0:T(128)}, f32[3,96,768]{2,1,0:T(8,128)}, f32[3,1,48]{2,1,0:T(1,128)}...) custom-call(bf16[512,1536]{1,0:T(8,128)(2,1)} %get-tuple-element.25.block_, ...), custom_call_target="tpu_custom_call" | custom-call | tf_op jit(solution)/shard_map/finish/pallas_call | solution.py:1145
